TPU v7x, 32 devices: a whole 2x2x4 slice. The times are simulated.
32 devices in a mesh: groups: 2 (over x), ctx: 16 (over z, y, core).
Axes of the slice: x: 2, y: 2, z: 4, core: 2. Of those that a mesh axis runs over, the one named last changes fastest.
Arguments:
- queries: bfloat16 [4096, 36864], P(('groups', 'ctx')), parts along dimension 0, may hold values from -48 to 48
- kv_cache: bfloat16 [4096, 576], P(('groups', 'ctx')), parts along dimension 0, may hold values from -4 to 4
- idx_queries: bfloat16 [4096, 4096], P(('groups', 'ctx')), parts along dimension 0, may hold values from -5 to 5
- idx_keys: bfloat16 [4096, 128], P(('groups', 'ctx')), parts along dimension 0, may hold values from -12 to 12
- idx_weights: float32 [4096, 32], P(('groups', 'ctx')), parts along dimension 0, may hold values from -1 to 1
- selected: int32 [4096, 2], P(('groups', 'ctx')), parts along dimension 0, may hold values from 0 to 15, as said below
- value_maps: bfloat16 [64, 512, 128], P('ctx'), may hold values from -0.25 to 0.25
Outputs:
- attended: bfloat16 [4096, 8192], P(('groups', 'ctx')), parts along dimension 0
- index_scores: float32 [4096, 16], P(('groups', 'ctx')), parts along dimension 0
There are 2 independent parts, one for each index of `groups`. A program takes and returns all parts, laid end to end along the dimension named above; an argument that names none is the same for every part. Nothing has to cross between parts.
Inputs may be any that keep to these rules, and one draw needn't show every extreme that they name: selected[t, 0] = t // 128; for 1 <= k <= t // 128, slot k names a block below t // 128, all of them distinct; slots k > t // 128 hold block numbers that are not used.
All inputs are finite; a program needn't handle non-finite values.
Results may differ from a plain program's by a relative error of at most 0.0058.
Values may be sent and summed in bfloat16 or wider, within the bound.
No kernel may reach another device: no remote copies, remote signals or barrier semaphores. Data moves between devices by JAX's collectives and lax.ppermute only.
A program may use at most 384 MiB of HBM per device.

v0:
```python
import math

import jax
import jax.numpy as jnp
from jax import lax
from jax.sharding import PartitionSpec as P

H = 64
DL = 512
DR = 64
DV = 128
HI = 32
DI = 128
BLK = 128
TOPB = 2


score_scale = 192.0 ** (-0.5)


def on_device(queries, kv_cache, idx_queries, idx_keys, idx_weights, selected, value_maps):
    row_count = queries.shape[0]
    row_width = kv_cache.shape[1]
    all_tokens = row_count * lax.axis_size("ctx")
    block_count = all_tokens // BLK
    first_row = lax.axis_index("ctx") * row_count
    positions = first_row + jnp.arange(row_count, dtype=jnp.int32)
    flat_queries = idx_queries.reshape(row_count * HI, DI)

    def tile_scores(key_rows):
        extent = key_rows.shape[0]
        logits = jnp.einsum(
            "qd,kd->qk", flat_queries, key_rows, preferred_element_type=jnp.float32
        ).astype(jnp.bfloat16)
        active = jnp.maximum(logits.astype(jnp.float32), 0.0).reshape(row_count, HI, extent)
        relevance = jnp.einsum(
            "rh,rhk->rk", idx_weights, active, precision=lax.Precision.HIGHEST
        ) * DI ** (-0.5)
        key_pos = jnp.arange(extent, dtype=jnp.int32)
        relevance = jnp.where(key_pos[None, :] <= positions[:, None], relevance, 0.0)
        onehot = (
            key_pos[:, None] // BLK == jnp.arange(block_count, dtype=jnp.int32)[None, :]
        ).astype(jnp.float32)
        return jnp.dot(relevance, onehot, precision=lax.Precision.HIGHEST)

    empty_sums = jnp.zeros((row_count, block_count), jnp.float32)
    key_rows = lax.all_gather(idx_keys, "ctx", axis=0, tiled=True)
    block_sums = lax.cond(
        jnp.int32(0) > first_row + row_count - 1, lambda: empty_sums, lambda: tile_scores(key_rows)
    )
    whole_cache = lax.all_gather(kv_cache, "ctx", axis=0, tiled=True)
    counts = jnp.clip(
        positions[:, None] - BLK * jnp.arange(block_count, dtype=jnp.int32)[None, :] + 1, 0, BLK
    ).astype(jnp.float32)
    index_scores = block_sums / jnp.maximum(counts, 1.0)
    cache_blocks = whole_cache.reshape(block_count, BLK, row_width)
    group_size = math.gcd(16, row_count)

    def attend(inputs):
        query_rows, chosen, row_pos = inputs
        key_pos = chosen[:, :, None] * BLK + jnp.arange(BLK, dtype=jnp.int32)[None, None, :]
        slot_ok = (
            jnp.arange(TOPB, dtype=jnp.int32)[None, :, None] <= (row_pos // BLK)[:, None, None]
        )
        usable = (slot_ok & (key_pos <= row_pos[:, None, None])).reshape(group_size, TOPB * BLK)
        key_rows = jnp.take(cache_blocks, chosen, axis=0).reshape(group_size, TOPB * BLK, row_width)
        scores = (
            jnp.einsum("ghd,gkd->ghk", query_rows, key_rows, preferred_element_type=jnp.float32)
            * score_scale
        )
        scores = jnp.where(usable[:, None, :], scores, -jnp.inf)
        row_max = jnp.max(scores, axis=-1, keepdims=True)
        expd = jnp.exp(scores - row_max)
        weights = (expd / jnp.sum(expd, axis=-1, keepdims=True)).astype(jnp.bfloat16)
        return jnp.einsum(
            "ghk,gkd->ghd", weights, key_rows[:, :, :DL], preferred_element_type=jnp.float32
        ).astype(jnp.bfloat16)

    latent_out = lax.map(
        attend,
        (
            queries.reshape(-1, group_size, H, DL + DR),
            selected.reshape(-1, group_size, TOPB),
            positions.reshape(-1, group_size),
        ),
    ).reshape(row_count, H, DL)
    attended = jnp.einsum(
        "thd,hde->the",
        latent_out,
        lax.all_gather(value_maps, "ctx", axis=0, tiled=True),
        preferred_element_type=jnp.float32,
    ).astype(jnp.bfloat16)
    return (attended.reshape(row_count, H * DV), index_scores)


def solution(mesh):
    return jax.shard_map(
        on_device,
        mesh=mesh,
        in_specs=(
            P(("groups", "ctx"), None),
            P(("groups", "ctx"), None),
            P(("groups", "ctx"), None),
            P(("groups", "ctx"), None),
            P(("groups", "ctx"), None),
            P(("groups", "ctx"), None),
            P("ctx", None, None),
        ),
        out_specs=(P(("groups", "ctx"), None), P(("groups", "ctx"), None)),
        check_vma=False,
    )
```

profile of v0, /device:TPU:1, one launch (start us, length us, event | category | flops | bytes accessed | tf_op | source)
XLA Modules:
  0.0 279.3 jit_solution(2828082992125536275)
XLA Ops:
  8.7 25.1 %all_gather.11 = bf16[2048,128]{1,0:T(8,128)(2,1)S(1)} all-gather(bf16[128,128]{1,0:T(8,128)(2,1)} %param.14), channel_id=1, replica_groups=mesh['groups'=2,'ctx'=16] {'ctx'}, dimensions={0}, use_global_device_ids=true | all-gather | bytes 557056 | tf_op jit(solution)/shard_map/all_gather | solution.py:47
  33.9 18.6 %reshape.246 = bf16[8,16,64,576]{3,2,1,0:T(8,128)(2,1)} reshape(bf16[128,36864]{1,0:T(8,128)(2,1)} %param.11) | data formatting | bytes 18874368 | tf_op jit(solution)/shard_map/reshape | solution.py:82
  52.5 36.9 %conditional.1 = (f32[128,16]{0,1:T(8,128)S(1)}) conditional(s32[]{:T(128)} %convert_element_type.33, (s32[]{:T(128)}, s32[128]{0:T(128)S(1)}, bf16[128,4096]{1,0:T(8,128)(2,1)S(1)}, bf16[2048,128]{1,0:T(8,128)(2,1)S(1)}, f32[128,32]{0,1:T(8,128)S(1)}) %tuple.60, () %tuple.28), branch_computations={%region_4.5_spmd, %region_5.6_spmd} | conditional | flops 2324480000 | bytes 72951304 | solution.py:48
  53.1 13.7 %convert_maximum_fusion = f32[4096,2048]{1,0:T(8,128)} fusion(bf16[4096,128]{1,0:T(8,128)(2,1)S(1)} %reshape.238, bf16[2048,128]{1,0:T(8,128)(2,1)S(1)} %get-tuple-element.96), kind=kOutput, calls=%fused_computation.1 | convolution fusion | flops 2172649472 | bytes 35127296 | tf_op jit(solution)/shard_map/cond/branch_0_fun/qd,kd->qk/dot_general | solution.py:32
  66.8 21.0 %fusion.43 = f32[128,1,2048]{2,1,0:T(1,128)S(1)} fusion(f32[128,32,2048]{2,1,0:T(8,128)} %bitcast.90, f32[128,32,1]{1,2,0:T(1,128)S(1)} %copy.40), kind=kOutput, calls=%fused_computation.65 | convolution fusion | flops 100663296 | bytes 34619392 | tf_op jit(solution)/shard_map/cond/branch_0_fun/rh,rhk->rk/dot_general | solution.py:36
  90.1 3.2 %copy.34 = bf16[2048,576]{1,0:T(8,128)(2,1)S(1)} copy(bf16[2048,576]{0,1:T(8,128)(2,1)} %all-gather.3.cloned.1.call-done) | data formatting | bytes 4718592 | tf_op jit(solution)/shard_map/all_gather | solution.py:51
  93.2 164.7 %while.12 = (s32[]{:T(128)}, bf16[8,16,64,512]{3,2,1,0:T(8,128)(2,1)}, s32[8,16]{1,0:T(8,128)S(1)}, s32[8,16,2]{1,0,2:T(8,128)S(1)}, bf16[8,16,64,576]{3,2,1,0:T...) while((s32[]{:T(128)}, bf16[8,16,64,512]{3,2,1,0:T(8,128)(2,1)}, s32[8,16]{1,0:T(8,128)S(1)}, ...), condition=%wide.region_3.4_spmd, body=%wide.region_0.3_spmd.sunk | while | flops 575159424 | bytes 57493132 | solution.py:79
  94.1 3.5 %gather_fusion = bf16[32,128,576]{2,1,0:T(8,128)(2,1)} fusion(bf16[16,128,576]{2,1,0:T(8,128)(2,1)S(1)} %get-tuple-element.213, s32[1024]{0:T(1024)S(1)} %pad_clamp_fusion.2), kind=kCustom, calls=%fused_computation.clone.1 | custom fusion | bytes 9437312 | tf_op jit(solution)/shard_map/while/body/eval_jaxpr/jit(_take)/gather | solution.py:66
  97.8 3.7 %bitcast_select_fusion.2 = bf16[16,256,576]{2,1,0:T(8,128)(2,1)S(1)} fusion(pred[16,256]{1,0:T(8,128)(4,1)S(1)} %bitcast.95, bf16[16,256,576]{2,1,0:T(8,128)(2,1)} %bitcast.88), kind=kLoop, calls=%fused_computation.23.clone.1 | loop fusion | flops 2359296 | bytes 9441280 | tf_op jit(solution)/shard_map/while/body/eval_jaxpr/jit(_take)/select_n | solution.py:66
  108.2 5.8 %fusion.69 = bf16[8,16,64,512]{3,2,1,0:T(8,128)(2,1)} fusion(bf16[8,16,64,512]{3,2,1,0:T(8,128)(2,1)} %get-tuple-element.202, s32[]{:T(128)} %get-tuple-element.201, bf16[16,256,576]{2,1,0:T(8,128)(2,1)} %copy-done, f32[16,64]{1,0:T(8,128)S(1)} %fusion.68, f32[16,64,256]{2,1,0:T(8,128)} %copy-done.1), kind=kOutput, calls=%fused_computation.32.clone.1 | convolution fusion | flops 269747456 | bytes 7344640 | tf_op jit(solution)/shard_map/while/body/eval_jaxpr/ghk,gkd->ghd/dot_general | solution.py:75
  114.7 3.5 %gather_fusion = bf16[32,128,576]{2,1,0:T(8,128)(2,1)} fusion(bf16[16,128,576]{2,1,0:T(8,128)(2,1)S(1)} %get-tuple-element.213, s32[1024]{0:T(1024)S(1)} %pad_clamp_fusion.2), kind=kCustom, calls=%fused_computation.clone.1 | custom fusion | bytes 9437312 | tf_op jit(solution)/shard_map/while/body/eval_jaxpr/jit(_take)/gather | solution.py:66
  118.4 3.7 %bitcast_select_fusion.2 = bf16[16,256,576]{2,1,0:T(8,128)(2,1)S(1)} fusion(pred[16,256]{1,0:T(8,128)(4,1)S(1)} %bitcast.95, bf16[16,256,576]{2,1,0:T(8,128)(2,1)} %bitcast.88), kind=kLoop, calls=%fused_computation.23.clone.1 | loop fusion | flops 2359296 | bytes 9441280 | tf_op jit(solution)/shard_map/while/body/eval_jaxpr/jit(_take)/select_n | solution.py:66
  128.8 5.9 %fusion.69 = bf16[8,16,64,512]{3,2,1,0:T(8,128)(2,1)} fusion(bf16[8,16,64,512]{3,2,1,0:T(8,128)(2,1)} %get-tuple-element.202, s32[]{:T(128)} %get-tuple-element.201, bf16[16,256,576]{2,1,0:T(8,128)(2,1)} %copy-done, f32[16,64]{1,0:T(8,128)S(1)} %fusion.68, f32[16,64,256]{2,1,0:T(8,128)} %copy-done.1), kind=kOutput, calls=%fused_computation.32.clone.1 | convolution fusion | flops 269747456 | bytes 7344640 | tf_op jit(solution)/shard_map/while/body/eval_jaxpr/ghk,gkd->ghd/dot_general | solution.py:75
  135.4 3.5 %gather_fusion = bf16[32,128,576]{2,1,0:T(8,128)(2,1)} fusion(bf16[16,128,576]{2,1,0:T(8,128)(2,1)S(1)} %get-tuple-element.213, s32[1024]{0:T(1024)S(1)} %pad_clamp_fusion.2), kind=kCustom, calls=%fused_computation.clone.1 | custom fusion | bytes 9437312 | tf_op jit(solution)/shard_map/while/body/eval_jaxpr/jit(_take)/gather | solution.py:66
  139.1 3.7 %bitcast_select_fusion.2 = bf16[16,256,576]{2,1,0:T(8,128)(2,1)S(1)} fusion(pred[16,256]{1,0:T(8,128)(4,1)S(1)} %bitcast.95, bf16[16,256,576]{2,1,0:T(8,128)(2,1)} %bitcast.88), kind=kLoop, calls=%fused_computation.23.clone.1 | loop fusion | flops 2359296 | bytes 9441280 | tf_op jit(solution)/shard_map/while/body/eval_jaxpr/jit(_take)/select_n | solution.py:66
  149.5 5.8 %fusion.69 = bf16[8,16,64,512]{3,2,1,0:T(8,128)(2,1)} fusion(bf16[8,16,64,512]{3,2,1,0:T(8,128)(2,1)} %get-tuple-element.202, s32[]{:T(128)} %get-tuple-element.201, bf16[16,256,576]{2,1,0:T(8,128)(2,1)} %copy-done, f32[16,64]{1,0:T(8,128)S(1)} %fusion.68, f32[16,64,256]{2,1,0:T(8,128)} %copy-done.1), kind=kOutput, calls=%fused_computation.32.clone.1 | convolution fusion | flops 269747456 | bytes 7344640 | tf_op jit(solution)/shard_map/while/body/eval_jaxpr/ghk,gkd->ghd/dot_general | solution.py:75
  155.9 3.5 %gather_fusion = bf16[32,128,576]{2,1,0:T(8,128)(2,1)} fusion(bf16[16,128,576]{2,1,0:T(8,128)(2,1)S(1)} %get-tuple-element.213, s32[1024]{0:T(1024)S(1)} %pad_clamp_fusion.2), kind=kCustom, calls=%fused_computation.clone.1 | custom fusion | bytes 9437312 | tf_op jit(solution)/shard_map/while/body/eval_jaxpr/jit(_take)/gather | solution.py:66
  159.6 3.7 %bitcast_select_fusion.2 = bf16[16,256,576]{2,1,0:T(8,128)(2,1)S(1)} fusion(pred[16,256]{1,0:T(8,128)(4,1)S(1)} %bitcast.95, bf16[16,256,576]{2,1,0:T(8,128)(2,1)} %bitcast.88), kind=kLoop, calls=%fused_computation.23.clone.1 | loop fusion | flops 2359296 | bytes 9441280 | tf_op jit(solution)/shard_map/while/body/eval_jaxpr/jit(_take)/select_n | solution.py:66
  170.0 5.7 %fusion.69 = bf16[8,16,64,512]{3,2,1,0:T(8,128)(2,1)} fusion(bf16[8,16,64,512]{3,2,1,0:T(8,128)(2,1)} %get-tuple-element.202, s32[]{:T(128)} %get-tuple-element.201, bf16[16,256,576]{2,1,0:T(8,128)(2,1)} %copy-done, f32[16,64]{1,0:T(8,128)S(1)} %fusion.68, f32[16,64,256]{2,1,0:T(8,128)} %copy-done.1), kind=kOutput, calls=%fused_computation.32.clone.1 | convolution fusion | flops 269747456 | bytes 7344640 | tf_op jit(solution)/shard_map/while/body/eval_jaxpr/ghk,gkd->ghd/dot_general | solution.py:75
  176.4 3.5 %gather_fusion = bf16[32,128,576]{2,1,0:T(8,128)(2,1)} fusion(bf16[16,128,576]{2,1,0:T(8,128)(2,1)S(1)} %get-tuple-element.213, s32[1024]{0:T(1024)S(1)} %pad_clamp_fusion.2), kind=kCustom, calls=%fused_computation.clone.1 | custom fusion | bytes 9437312 | tf_op jit(solution)/shard_map/while/body/eval_jaxpr/jit(_take)/gather | solution.py:66
  180.1 3.7 %bitcast_select_fusion.2 = bf16[16,256,576]{2,1,0:T(8,128)(2,1)S(1)} fusion(pred[16,256]{1,0:T(8,128)(4,1)S(1)} %bitcast.95, bf16[16,256,576]{2,1,0:T(8,128)(2,1)} %bitcast.88), kind=kLoop, calls=%fused_computation.23.clone.1 | loop fusion | flops 2359296 | bytes 9441280 | tf_op jit(solution)/shard_map/while/body/eval_jaxpr/jit(_take)/select_n | solution.py:66
  190.5 5.8 %fusion.69 = bf16[8,16,64,512]{3,2,1,0:T(8,128)(2,1)} fusion(bf16[8,16,64,512]{3,2,1,0:T(8,128)(2,1)} %get-tuple-element.202, s32[]{:T(128)} %get-tuple-element.201, bf16[16,256,576]{2,1,0:T(8,128)(2,1)} %copy-done, f32[16,64]{1,0:T(8,128)S(1)} %fusion.68, f32[16,64,256]{2,1,0:T(8,128)} %copy-done.1), kind=kOutput, calls=%fused_computation.32.clone.1 | convolution fusion | flops 269747456 | bytes 7344640 | tf_op jit(solution)/shard_map/while/body/eval_jaxpr/ghk,gkd->ghd/dot_general | solution.py:75
  196.9 3.5 %gather_fusion = bf16[32,128,576]{2,1,0:T(8,128)(2,1)} fusion(bf16[16,128,576]{2,1,0:T(8,128)(2,1)S(1)} %get-tuple-element.213, s32[1024]{0:T(1024)S(1)} %pad_clamp_fusion.2), kind=kCustom, calls=%fused_computation.clone.1 | custom fusion | bytes 9437312 | tf_op jit(solution)/shard_map/while/body/eval_jaxpr/jit(_take)/gather | solution.py:66
  200.6 3.7 %bitcast_select_fusion.2 = bf16[16,256,576]{2,1,0:T(8,128)(2,1)S(1)} fusion(pred[16,256]{1,0:T(8,128)(4,1)S(1)} %bitcast.95, bf16[16,256,576]{2,1,0:T(8,128)(2,1)} %bitcast.88), kind=kLoop, calls=%fused_computation.23.clone.1 | loop fusion | flops 2359296 | bytes 9441280 | tf_op jit(solution)/shard_map/while/body/eval_jaxpr/jit(_take)/select_n | solution.py:66
  211.1 5.8 %fusion.69 = bf16[8,16,64,512]{3,2,1,0:T(8,128)(2,1)} fusion(bf16[8,16,64,512]{3,2,1,0:T(8,128)(2,1)} %get-tuple-element.202, s32[]{:T(128)} %get-tuple-element.201, bf16[16,256,576]{2,1,0:T(8,128)(2,1)} %copy-done, f32[16,64]{1,0:T(8,128)S(1)} %fusion.68, f32[16,64,256]{2,1,0:T(8,128)} %copy-done.1), kind=kOutput, calls=%fused_computation.32.clone.1 | convolution fusion | flops 269747456 | bytes 7344640 | tf_op jit(solution)/shard_map/while/body/eval_jaxpr/ghk,gkd->ghd/dot_general | solution.py:75
  217.5 3.5 %gather_fusion = bf16[32,128,576]{2,1,0:T(8,128)(2,1)} fusion(bf16[16,128,576]{2,1,0:T(8,128)(2,1)S(1)} %get-tuple-element.213, s32[1024]{0:T(1024)S(1)} %pad_clamp_fusion.2), kind=kCustom, calls=%fused_computation.clone.1 | custom fusion | bytes 9437312 | tf_op jit(solution)/shard_map/while/body/eval_jaxpr/jit(_take)/gather | solution.py:66
  221.2 3.7 %bitcast_select_fusion.2 = bf16[16,256,576]{2,1,0:T(8,128)(2,1)S(1)} fusion(pred[16,256]{1,0:T(8,128)(4,1)S(1)} %bitcast.95, bf16[16,256,576]{2,1,0:T(8,128)(2,1)} %bitcast.88), kind=kLoop, calls=%fused_computation.23.clone.1 | loop fusion | flops 2359296 | bytes 9441280 | tf_op jit(solution)/shard_map/while/body/eval_jaxpr/jit(_take)/select_n | solution.py:66
  231.6 5.7 %fusion.69 = bf16[8,16,64,512]{3,2,1,0:T(8,128)(2,1)} fusion(bf16[8,16,64,512]{3,2,1,0:T(8,128)(2,1)} %get-tuple-element.202, s32[]{:T(128)} %get-tuple-element.201, bf16[16,256,576]{2,1,0:T(8,128)(2,1)} %copy-done, f32[16,64]{1,0:T(8,128)S(1)} %fusion.68, f32[16,64,256]{2,1,0:T(8,128)} %copy-done.1), kind=kOutput, calls=%fused_computation.32.clone.1 | convolution fusion | flops 269747456 | bytes 7344640 | tf_op jit(solution)/shard_map/while/body/eval_jaxpr/ghk,gkd->ghd/dot_general | solution.py:75
  238.0 3.5 %gather_fusion = bf16[32,128,576]{2,1,0:T(8,128)(2,1)} fusion(bf16[16,128,576]{2,1,0:T(8,128)(2,1)S(1)} %get-tuple-element.213, s32[1024]{0:T(1024)S(1)} %pad_clamp_fusion.2), kind=kCustom, calls=%fused_computation.clone.1 | custom fusion | bytes 9437312 | tf_op jit(solution)/shard_map/while/body/eval_jaxpr/jit(_take)/gather | solution.py:66
  241.7 3.7 %bitcast_select_fusion.2 = bf16[16,256,576]{2,1,0:T(8,128)(2,1)S(1)} fusion(pred[16,256]{1,0:T(8,128)(4,1)S(1)} %bitcast.95, bf16[16,256,576]{2,1,0:T(8,128)(2,1)} %bitcast.88), kind=kLoop, calls=%fused_computation.23.clone.1 | loop fusion | flops 2359296 | bytes 9441280 | tf_op jit(solution)/shard_map/while/body/eval_jaxpr/jit(_take)/select_n | solution.py:66
  252.1 5.8 %fusion.69 = bf16[8,16,64,512]{3,2,1,0:T(8,128)(2,1)} fusion(bf16[8,16,64,512]{3,2,1,0:T(8,128)(2,1)} %get-tuple-element.202, s32[]{:T(128)} %get-tuple-element.201, bf16[16,256,576]{2,1,0:T(8,128)(2,1)} %copy-done, f32[16,64]{1,0:T(8,128)S(1)} %fusion.68, f32[16,64,256]{2,1,0:T(8,128)} %copy-done.1), kind=kOutput, calls=%fused_computation.32.clone.1 | convolution fusion | flops 269747456 | bytes 7344640 | tf_op jit(solution)/shard_map/while/body/eval_jaxpr/ghk,gkd->ghd/dot_general | solution.py:75
  257.9 11.7 %fusion.38 = bf16[64,128,128]{1,2,0:T(8,128)(2,1)S(1)} fusion(bf16[64,512,128]{2,1,0:T(8,128)(2,1)} %all-gather.5.cloned.1.call-done, bf16[128,64,512]{2,1,0:T(8,128)(2,1)} %bitcast.100), kind=kOutput, calls=%fused_computation.59 | convolution fusion | flops 1074790400 | bytes 18874368 | tf_op jit(solution)/shard_map/thd,hde->the/dot_general | solution.py:87
  (209 shorter events, 67.1 us)
Async XLA Ops:
  7.2 82.9 %all-gather.3.cloned.1.call-start = ((), (), s32[]{:S(2)}) async-start(), calls=%async_computation | async-start | bytes 2506752 | tf_op jit(solution)/shard_map/all_gather | solution.py:51
  7.9 250.0 %all-gather.5.cloned.1.call-start = ((), (), s32[]{:S(2)}) async-start(), calls=%async_computation.1 | async-start | bytes 8912896 | tf_op jit(solution)/shard_map/all_gather | solution.py:90
  33.8 18.6 %copy-start.4 = (s32[128,2]{0,1:T(2,128)S(1)}, s32[128,2]{0,1:T(2,128)}, u32[]{:S(2)}) copy-start(s32[128,2]{0,1:T(2,128)} %param.16) | copy-start | bytes 3076
  33.9 18.7 %copy-start.2 = (bf16[128,4096]{1,0:T(8,128)(2,1)S(1)}, bf16[128,4096]{1,0:T(8,128)(2,1)}, u32[]{:S(2)}) copy-start(bf16[128,4096]{1,0:T(8,128)(2,1)} %param.13) | copy-start | bytes 3145732
  33.9 18.7 %copy-start.3 = (f32[128,32]{0,1:T(8,128)S(1)}, f32[128,32]{0,1:T(8,128)}, u32[]{:S(2)}) copy-start(f32[128,32]{0,1:T(8,128)} %param.15) | copy-start | bytes 49156
  101.5 2.3 copy-start
  106.9 1.0 copy-start.1
  122.1 2.3 copy-start
  127.5 1.0 copy-start.1
  142.8 2.3 copy-start
  148.2 1.0 copy-start.1
  163.3 2.3 copy-start
  168.7 1.0 copy-start.1
  183.8 2.3 copy-start
  189.2 1.0 copy-start.1
  204.3 2.3 copy-start
  209.7 1.0 copy-start.1
  224.9 2.3 copy-start
  230.3 1.0 copy-start.1
  245.4 2.3 copy-start
  250.8 1.0 copy-start.1
Sparse Core Ops, SparseCore 0:
  10.2 46.1 all-gather.2
  58.5 73.5 all-gather.4
where the time goes:
time: 280 us; the launch traced here: 279 us
  matrix products  119 us (42%)
  local copies, waits for them, and re-layouts  84.4 us (30%)
  other arithmetic  34.6 us (12%)
  blocking collectives  25.1 us (9%)
  between operations  14.1 us (5%)
    dot_general x8, matrix products, attend(): jnp.einsum('ghk,gkd->ghd', weights, key_rows[:, :, :DL], preferred_elemen...  46.3 us
    select_n x16, other arithmetic, attend(): jnp.take(cache_blocks, chosen, axis=0)  29.7 us
    gather x8, local copies, waits for them, and re-layouts, attend(): jnp.take(cache_blocks, chosen, axis=0)  28 us
    while x40, local copies, waits for them, and re-layouts  26.2 us
    all_gather x1, blocking collectives, on_device(): key_rows = lax.all_gather(idx_keys, 'ctx', axis=0, tiled=True)  25.1 us
    dot_general x8, matrix products, attend(): jnp.einsum('ghd,gkd->ghk', query_rows, key_rows, preferred_element_type=j...  24.5 us
    dot_general x1, matrix products, tile_scores(): jnp.einsum('rh,rhk->rk', idx_weights, active, precision=lax.Precision.HIG...  21 us
    reshape x1, local copies, waits for them, and re-layouts, on_device(): queries.reshape(-1, group_size, H, DL + DR)  18.6 us
  transfers between devices with their start and end apart: 2, of which 0 were waited for; matrix products, arithmetic and copies ran while one was open for 71% of the time, Pallas kernels for 0%

commit v1 on v0

v1 whole, which is shorter than its diff:
```python
import functools
import math

import jax
import jax.numpy as jnp
from jax import lax
from jax.experimental import pallas as pl
from jax.experimental.pallas import tpu as pltpu
from jax.sharding import PartitionSpec as P

H = 64
DL = 512
DR = 64
DV = 128
HI = 32
DI = 128
BLK = 128
WIN = 16
DQ = DL + DR
PACK = DI + DQ

exponent_scale = 192.0 ** (-0.5) * math.log2(math.e)
f32 = jnp.float32
bf16 = jnp.bfloat16
SMALL = pl.CostEstimate(flops=1, bytes_accessed=1, transcendentals=0)


def sort_kernel(order_ref, q_ref, out_ref):
    heads = out_ref.shape[1]
    windows = out_ref.shape[0]
    rows = jnp.dot(order_ref[...], q_ref[...], preferred_element_type=f32)
    for h in range(heads):
        part = rows[:, h * DQ : (h + 1) * DQ].astype(bf16)
        out_ref[:, h] = part.reshape(windows, WIN, DQ)


def sort_queries(order, queries):
    count = queries.shape[0]
    step = 16
    return pl.pallas_call(
        sort_kernel,
        grid=(H // step,),
        in_specs=[
            pl.BlockSpec((count, count), lambda i: (0, 0)),
            pl.BlockSpec((count, step * DQ), lambda i: (0, i)),
        ],
        out_specs=pl.BlockSpec((count // WIN, step, WIN, DQ), lambda i: (0, i, 0, 0)),
        out_shape=jax.ShapeDtypeStruct((count // WIN, H, WIN, DQ), bf16),
        compiler_params=pltpu.CompilerParams(vmem_limit_bytes=48 * 2**20),
        cost_estimate=SMALL,
        name="sort_queries",
    )(order, queries)


def with_block(pieces, place, use):
    size = pieces[0].shape[0]
    if len(pieces) == 1:
        use(pieces[0].at[place])
        return
    for k, piece in enumerate(pieces):

        @pl.when(place // size == k)
        def _():
            use(piece.at[lax.rem(place, size)])


def place_of(relative, j, me):
    if not relative:
        return j
    other = j ^ me
    return (other & 1) * 8 + ((other >> 1) & 1) * 4 + (other >> 2)


def attend_kernel(relative, count, first_ref, key_ref, me_ref, q_ref, pos_ref, keys_ref, *refs):
    pieces = refs[:count]
    out_ref, rhs_ref = refs[count:]
    w = pl.program_id(0)
    me = me_ref[0]
    lo = w * WIN

    def load(j, column):
        def use(block):
            rhs_ref[:, column : column + BLK] = block[DI:PACK, :]

        with_block(pieces, place_of(relative, j, me), use)

    @pl.when(w == 0)
    def _():
        load(me, 0)

    column = lax.broadcasted_iota(jnp.int32, (WIN, 2 * BLK), 1)
    last = jnp.where(me > 0, 2 * BLK, 0)
    usable = (column <= pos_ref[...]) | ((column >= BLK) & (column < last))
    bias = jnp.where(usable, 0.0, -jnp.inf).astype(f32)
    keys = keys_ref[...]

    def block(j, carry):
        start = jnp.maximum(first_ref[j], lo)
        end = jnp.minimum(first_ref[j + 1], lo + WIN)

        @pl.when(end > start)
        def _():
            load(j, BLK)
            mine = (keys == j)[None]
            scores = jnp.dot(
                q_ref[0].reshape(H * WIN, DQ), rhs_ref[...], preferred_element_type=f32
            ).reshape(H, WIN, 2 * BLK) + bias[None]
            top = jnp.max(scores, axis=-1, keepdims=True)
            expd = jnp.exp2((scores - top) * exponent_scale)
            total = jnp.sum(expd, axis=-1, keepdims=True)
            weights = (expd * (1.0 / total)).astype(bf16)
            values = lax.dot_general(
                weights.reshape(H * WIN, 2 * BLK),
                rhs_ref[0:DL, :],
                (((1,), (1,)), ((), ())),
                preferred_element_type=f32,
            ).reshape(H, WIN, DL)
            old = out_ref[...].astype(f32)
            out_ref[...] = jnp.where(mine, values, old).astype(bf16)

        return carry

    lax.fori_loop(key_ref[lo], key_ref[lo + WIN - 1] + 1, block, 0)


def attend(relative, first, sorted_key, me, sorted_q, pieces, sorted_pos):
    count = sorted_key.shape[0]
    spec = pltpu.PrefetchScalarGridSpec(
        num_scalar_prefetch=3,
        grid=(count // WIN,),
        in_specs=[
            pl.BlockSpec((1, H, WIN, DQ), lambda w, *_: (w, 0, 0, 0)),
            pl.BlockSpec((WIN, 1), lambda w, *_: (w, 0)),
            pl.BlockSpec((WIN, 1), lambda w, *_: (w, 0)),
        ]
        + [pl.BlockSpec((p.shape[0], PACK, BLK), lambda w, *_: (0, 0, 0)) for p in pieces],
        out_specs=pl.BlockSpec((H, WIN, DL), lambda w, *_: (0, w, 0)),
        scratch_shapes=[pltpu.VMEM((DQ, 2 * BLK), bf16)],
    )
    return pl.pallas_call(
        functools.partial(attend_kernel, relative, len(pieces)),
        grid_spec=spec,
        out_shape=jax.ShapeDtypeStruct((H, count, DL), bf16),
        compiler_params=pltpu.CompilerParams(vmem_limit_bytes=48 * 2**20),
        cost_estimate=SMALL,
        name="attend",
    )(first, sorted_key, me, sorted_q, sorted_pos[:, None], sorted_key[:, None], *pieces)


def unit_place(unit, me_ref):
    device, half, relative = unit
    side = (me_ref[1] ^ half) if relative else half
    return (me_ref[0] ^ device) * 2 + side


def project_kernel(units, sizes, before_units, final, me_ref, *refs):
    back_ref = refs[0]
    latents = refs[1 : 1 + len(units)]
    pieces = refs[1 + len(units) : 1 + len(units) + len(sizes)]
    out_ref = refs[-1]
    if before_units:
        before_ref = refs[-2]
        for n, unit in enumerate(before_units):
            place = pl.multiple_of(unit_place(unit, me_ref) * 2 * DV, 2 * DV)
            out_ref[:, pl.ds(place, 2 * DV)] = before_ref[:, n * 2 * DV : (n + 1) * 2 * DV]
    n = 0
    parts = []
    for piece, size in zip(pieces, sizes):
        for k in range(size):
            parts.append(
                jnp.dot(latents[n // 2][n % 2], piece[k], preferred_element_type=f32).astype(bf16)
            )
            n += 1
    rows = jnp.dot(
        back_ref[...], jnp.concatenate(parts, axis=1), preferred_element_type=f32
    ).astype(bf16)
    if not final:
        out_ref[...] = rows
        return
    for n, unit in enumerate(units):
        place = pl.multiple_of(unit_place(unit, me_ref) * 2 * DV, 2 * DV)
        out_ref[:, pl.ds(place, 2 * DV)] = rows[:, n * 2 * DV : (n + 1) * 2 * DV]


def project(me, back, latents, units, pieces, before_units=(), before=None, final=False):
    count = latents.shape[1]
    sizes = tuple(p.shape[0] for p in pieces)
    width = H * DV if final else len(units) * 2 * DV

    def latent_spec(unit):
        return pl.BlockSpec((2, count, DL), lambda i, me_ref: (unit_place(unit, me_ref), 0, 0))

    in_specs = [pl.BlockSpec((count, count), lambda i, m: (0, 0))]
    in_specs += [latent_spec(unit) for unit in units]
    in_specs += [pl.BlockSpec((n, DL, DV), lambda i, m: (0, 0, 0)) for n in sizes]
    operands = [me, back] + [latents] * len(units) + list(pieces)
    if before is not None:
        in_specs.append(pl.BlockSpec(before.shape, lambda i, m: (0, 0)))
        operands.append(before)
    spec = pltpu.PrefetchScalarGridSpec(
        num_scalar_prefetch=1,
        grid=(1,),
        in_specs=in_specs,
        out_specs=pl.BlockSpec((count, width), lambda i, m: (0, 0)),
    )
    return pl.pallas_call(
        functools.partial(project_kernel, tuple(units), sizes, tuple(before_units), final),
        grid_spec=spec,
        out_shape=jax.ShapeDtypeStruct((count, width), bf16),
        compiler_params=pltpu.CompilerParams(vmem_limit_bytes=56 * 2**20),
        cost_estimate=SMALL,
        name="project",
    )(*operands)


def index_kernel(relative, count, me_ref, q_ref, w_ref, *refs):
    pieces = refs[:count]
    out_ref, acc_ref, keys_ref = refs[count:]
    me = me_ref[0]
    rows = q_ref.shape[0]
    acc_ref[...] = jnp.zeros_like(acc_ref)
    row = lax.broadcasted_iota(jnp.int32, (BLK, rows), 0)
    col = lax.broadcasted_iota(jnp.int32, (BLK, rows), 1)

    def block(j, mask):
        def use(piece):
            keys_ref[...] = piece[...]

        with_block(pieces, place_of(relative, j, me), use)
        keys = keys_ref[...]
        total = jnp.zeros((8, rows), f32)
        for h in range(0, HI, 2):
            pair = jnp.concatenate(
                [q_ref[:, h * DI : (h + 1) * DI], q_ref[:, (h + 1) * DI : (h + 2) * DI]], axis=0
            )
            logits = lax.dot_general(keys, pair, (((1,), (1,)), ((), ())), preferred_element_type=f32)
            active = jnp.maximum(logits, 0.0)
            for k in range(2):
                half = active[:, k * rows : (k + 1) * rows]
                if mask is not None:
                    half = jnp.where(mask, half, 0.0)
                sums = jnp.sum(half.reshape(BLK // 8, 8, rows), axis=0)
                total = total + sums * w_ref[h + k : h + k + 1, :]
        acc_ref[pl.ds(j, 1), :] = jnp.sum(total, axis=0, keepdims=True)

    def step(j, carry):
        block(j, None)
        return carry

    lax.fori_loop(0, me, step, 0)
    block(me, row <= col)
    blocks = out_ref.shape[1]
    sums = acc_ref[...].T[:, 0:blocks]
    position = me * BLK + lax.broadcasted_iota(jnp.int32, (rows, blocks), 0)
    block_first = BLK * lax.broadcasted_iota(jnp.int32, (rows, blocks), 1)
    counts = jnp.clip(position - block_first + 1, 1, BLK).astype(f32)
    out_ref[...] = sums * (DI ** (-0.5)) / counts


def index_scores(relative, me, idx_queries, weights_t, pieces):
    count = idx_queries.shape[0]
    blocks = sum(p.shape[0] for p in pieces)
    rows = -(-blocks // 128) * 128
    spec = pltpu.PrefetchScalarGridSpec(
        num_scalar_prefetch=1,
        grid=(1,),
        in_specs=[
            pl.BlockSpec((count, HI * DI), lambda i, *_: (0, 0)),
            pl.BlockSpec((HI, count), lambda i, *_: (0, 0)),
        ]
        + [pl.BlockSpec((p.shape[0], BLK, DI), lambda i, *_: (0, 0, 0)) for p in pieces],
        out_specs=pl.BlockSpec((count, blocks), lambda i, *_: (0, 0)),
        scratch_shapes=[pltpu.VMEM((rows, count), f32), pltpu.VMEM((BLK, DI), bf16)],
    )
    return pl.pallas_call(
        functools.partial(index_kernel, relative, len(pieces)),
        grid_spec=spec,
        out_shape=jax.ShapeDtypeStruct((count, blocks), f32),
        compiler_params=pltpu.CompilerParams(vmem_limit_bytes=48 * 2**20),
        cost_estimate=SMALL,
        name="index_scores",
    )(me, idx_queries, weights_t, *pieces)


def on_ctx(me_to, devices=16):
    return [(i, me_to(i)) for i in range(devices)]


def over_z(k):
    return on_ctx(lambda i: i ^ (4 * k))


OVER_Y = on_ctx(lambda i: i ^ 2)
OVER_CORE = on_ctx(lambda i: i ^ 1)
OVER_XY = [(g * 16 + i, (1 - g) * 16 + (i ^ 2)) for g in range(2) for i in range(16)]


def along(array, pairs):
    return lax.ppermute(array, "ctx", pairs)


def after(array, *others):
    return lax.optimization_barrier((array,) + others)[0]


def on_device(queries, kv_cache, idx_queries, idx_keys, idx_weights, selected, value_maps):
    count = queries.shape[0]
    devices = lax.axis_size("ctx")
    blocks = count * devices // BLK
    assert count == BLK
    me = lax.axis_index("ctx")
    x = lax.axis_index("groups")
    meta = jnp.stack([me, x]).astype(jnp.int32)
    pack = jnp.concatenate([idx_keys, kv_cache.T], axis=0)
    relative = devices == 16 and lax.axis_size("groups") == 2 and value_maps.shape[0] == 4

    if relative:
        half = lax.dynamic_slice_in_dim(value_maps, 2 * x, 2, 0)
        pack_1, pack_2 = along(pack, over_z(1)), along(pack, over_z(2))
        half_1, half_2 = along(half, over_z(1)), along(half, over_z(2))
        from_y = along(value_maps, OVER_Y)
        pack_3 = along(pack_2, over_z(1))
        column_parts = [pack, pack_1, pack_2, pack_3]

    key = jnp.where(me > 0, selected[:, 1], 0)
    token = jnp.arange(count, dtype=jnp.int32)
    before = (key[:, None] < key[None, :]) | ((key[:, None] == key[None, :]) & (token[:, None] < token[None, :]))
    rank = jnp.sum(before.astype(jnp.int32), axis=0)
    order = rank[None, :] == token[:, None]
    back = order.T.astype(bf16)
    sorted_key = jnp.sum(jnp.where(order, key[None, :], 0), axis=1)
    sorted_pos = jnp.sum(jnp.where(order, token[None, :], 0), axis=1)
    first = jnp.sum(
        (key[None, :] < jnp.arange(blocks + 1, dtype=jnp.int32)[:, None]).astype(jnp.int32), axis=1
    )
    order = order.astype(bf16)
    if relative:
        order = after(order, pack_2)
    sorted_q = sort_queries(order, queries)

    if not relative:
        cache = lax.all_gather(pack, "ctx", axis=0, tiled=True).reshape(blocks, PACK, BLK)
        maps = lax.all_gather(value_maps, "ctx", axis=0, tiled=True)
        scores = index_scores(False, meta, idx_queries, idx_weights.T, [cache])
        latents = attend(False, first, sorted_key, meta, sorted_q, [cache], sorted_pos)
        meta = jnp.zeros_like(meta)
        parts = []
        for h in range(0, H, 16):
            units = [(u // 2, u % 2, False) for u in range(h // 2, h // 2 + 8)]
            parts.append(project(meta, back, latents, units, [maps[h : h + 16]]))
        return (jnp.concatenate(parts, axis=1), scores)

    half_3 = along(half_2, over_z(1))
    quarter_parts = [half_1, half_2, half_3]
    column = after(jnp.concatenate(column_parts, axis=0), sorted_q, half_2)
    column_y = along(column, OVER_Y)
    quarter = jnp.concatenate(quarter_parts, axis=0)
    quarter_x = lax.ppermute(quarter, "groups", [(0, 1), (1, 0)])
    quarter_y = along(quarter, OVER_Y)
    quarter_xy = lax.ppermute(quarter, ("groups", "ctx"), OVER_XY)
    pieces = [column, column_y, along(column, OVER_CORE), along(column_y, OVER_CORE)]
    pieces = [p.reshape(4, PACK, BLK) for p in pieces]
    pieces, quarter = lax.optimization_barrier((pieces, quarter))

    latents = attend(True, first, sorted_key, meta, sorted_q, pieces, sorted_pos)
    scores = index_scores(True, meta, idx_queries, idx_weights.T, pieces)

    def both_cores(arrays, units):
        arrays = list(arrays) + [along(a, OVER_CORE) for a in arrays]
        return arrays, units + [(device ^ 1, half, rel) for device, half, rel in units]

    early, early_units = both_cores(
        [value_maps, from_y, quarter],
        [(0, 0, False), (0, 1, False), (2, 0, False), (2, 1, False)] + [(4 * z, 0, True) for z in (1, 2, 3)],
    )
    early_out = project(meta, back, latents, early_units, early)
    late_in = [after(a, early_out) for a in (quarter_x, quarter_y, quarter_xy)]
    late, late_units = both_cores(
        late_in,
        [(4 * z, 1, True) for z in (1, 2, 3)]
        + [(4 * z + 2, 0, True) for z in (1, 2, 3)]
        + [(4 * z + 2, 1, True) for z in (1, 2, 3)],
    )
    attended = project(meta, back, latents, late_units, late, early_units, early_out, final=True)
    return (attended, scores)


def solution(mesh):
    return jax.shard_map(
        on_device,
        mesh=mesh,
        in_specs=(
            P(("groups", "ctx"), None),
            P(("groups", "ctx"), None),
            P(("groups", "ctx"), None),
            P(("groups", "ctx"), None),
            P(("groups", "ctx"), None),
            P(("groups", "ctx"), None),
            P("ctx", None, None),
        ),
        out_specs=(P(("groups", "ctx"), None), P(("groups", "ctx"), None)),
        check_vma=False,
    )
```

time: 280 us -> 132 us (0.47)
  the two profiles are of different devices: /device:TPU:1 before, /device:TPU:31 now
where the time goes in v1:
time: 132 us
  Pallas kernels  76.6 us (58%)
  waiting for transfers between devices  30.4 us (23%)
  starting transfers between devices  14.9 us (11%)
  local copies, waits for them, and re-layouts  6.61 us (5%)
  other arithmetic  2.69 us (2%)
    pallas_call x1, Pallas kernels, attend(): pl.pallas_call(functools.partial(attend_kernel, relative, len(pieces)), g...  45.1 us
    ppermute x17, waiting for transfers between devices, along(): return lax.ppermute(array, 'ctx', pairs)  30.4 us
    pallas_call x2, Pallas kernels, project(): pl.pallas_call(functools.partial(project_kernel, tuple(units), sizes, tup...  14 us
    ppermute x17, starting transfers between devices, along(): return lax.ppermute(array, 'ctx', pairs)  12.5 us
    pallas_call x1, Pallas kernels, sort_queries(): pl.pallas_call(sort_kernel, grid=(H // step,), in_specs=[pl.BlockSpec((co...  9.29 us
    pallas_call x1, Pallas kernels, index_scores(): pl.pallas_call(functools.partial(index_kernel, relative, len(pieces)), gr...  8.22 us
    unnamed x21, local copies, waits for them, and re-layouts  4.67 us
  transfers between devices with their start and end apart: 19, of which 5 were waited for; matrix products, arithmetic and copies ran while one was open for 6% of the time, Pallas kernels for 52%

profile of v1, /device:TPU:31, one launch (start us, length us, event | category | flops | bytes accessed | tf_op | source)
XLA Modules:
  0.0 132.0 jit_solution(14686789593487589176)
XLA Ops:
  0.6 0.9 pad_maximum_fusion
  1.9 1.0 constant_dynamic-slice_fusion
  2.8 2.4 %collective-permute-start.3 = (bf16[2,512,128]{2,1,0:T(8,128)(2,1)S(1)}, bf16[2,512,128]{2,1,0:T(8,128)(2,1)S(1)}, u32[]{:S(2)}, u32[]{:S(2)}) collective-permute-start(bf16[2,512,128]{2,1,0:T(8,128)(2,1)S(1)} %constant_dynamic-slice_fusion), channel_id=1, source_target_pairs={{0,8},{1,9},{2,10},{3,11},{4,12},{5,13},{6,14},{7,15},{8,0},{9,1},... | collective-permute-start | bytes 786440 | tf_op jit(solution)/shard_map/ppermute | solution.py:299
  5.2 0.8 constant_dynamic-update-slice_fusion.4
  6.0 0.7 fusion.4
  6.7 0.9 constant_dynamic-update-slice_fusion.3
  7.7 0.7 fusion
  8.4 5.4 %collective-permute-done = bf16[704,128]{1,0:T(8,128)(2,1)S(1)} collective-permute-done((bf16[704,128]{1,0:T(8,128)(2,1)S(1)}, bf16[704,128]{1,0:T(8,128)(2,1)S(1)}, u32[]{:S(2)}, u32[]{:S(2)}) %collective-permute-start) | collective-permute-done | bytes 180256 | tf_op jit(solution)/shard_map/ppermute | solution.py:299
  13.8 9.3 %sort_queries.1.q_ref = bf16[8,64,16,576]{3,2,1,0:T(8,128)(2,1)} custom-call(bf16[128,128]{1,0:T(8,128)(2,1)S(1)} %get-tuple-element.12.order_ref, bf16[128,36864]{1,0:T(8,128)(2,1)} %q_ref.2), custom_call_target="tpu_custom_call" | custom-call | flops 1 | bytes 1 | tf_op jit(solution)/shard_map/sort_queries/pallas_call | solution.py:40
  23.1 1.5 %collective-permute-done.2 = bf16[704,128]{1,0:T(8,128)(2,1)S(1)} collective-permute-done((bf16[704,128]{1,0:T(8,128)(2,1)S(1)}, bf16[704,128]{1,0:T(8,128)(2,1)S(1)}, u32[]{:S(2)}, u32[]{:S(2)}) %collective-permute-start.2) | collective-permute-done | bytes 180256 | tf_op jit(solution)/shard_map/ppermute | solution.py:299
  24.7 0.3 collective-permute-start.4
  25.0 1.8 %collective-permute-start.5 = (bf16[2816,128]{1,0:T(8,128)(2,1)S(1)}, bf16[2816,128]{1,0:T(8,128)(2,1)S(1)}, u32[]{:S(2)}, u32[]{:S(2)}) collective-permute-start(bf16[2816,128]{1,0:T(8,128)(2,1)S(1)} %constant_dynamic-update-slice_fusion), channel_id=1, source_target_pairs={{0,1},{1,0},{2,3},{3,2},{4,5},{5,4},{6,7},{7,6},{8,9},{9,8},{10,11... | collective-permute-start | bytes 2162696 | tf_op jit(solution)/shard_map/ppermute | solution.py:299
  26.8 14.0 %collective-permute-done.4 = bf16[2816,128]{1,0:T(8,128)(2,1)S(1)} collective-permute-done((bf16[2816,128]{1,0:T(8,128)(2,1)S(1)}, bf16[2816,128]{1,0:T(8,128)(2,1)S(1)}, u32[]{:S(2)}, u32[]{:S(2)}) %collective-permute-start.4) | collective-permute-done | bytes 720928 | tf_op jit(solution)/shard_map/ppermute | solution.py:299
  40.8 2.5 %collective-permute-start.6 = (bf16[2816,128]{1,0:T(8,128)(2,1)S(1)}, bf16[2816,128]{1,0:T(8,128)(2,1)S(1)}, u32[]{:S(2)}, u32[]{:S(2)}) collective-permute-start(bf16[2816,128]{1,0:T(8,128)(2,1)S(1)} %collective-permute-done.4), channel_id=1, source_target_pairs={{0,1},{1,0},{2,3},{3,2},{4,5},{5,4},{6,7},{7,6},{8,9},{9,8},{10,11... | collective-permute-start | bytes 2162696 | tf_op jit(solution)/shard_map/ppermute | solution.py:299
  43.5 1.5 %collective-permute-start.8 = (bf16[2,512,128]{2,1,0:T(8,128)(2,1)S(1)}, bf16[2,512,128]{2,1,0:T(8,128)(2,1)S(1)}, u32[]{:S(2)}, u32[]{:S(2)}) collective-permute-start(bf16[2,512,128]{2,1,0:T(8,128)(2,1)S(1)} %collective-permute-done.3), channel_id=1, source_target_pairs={{0,4},{1,5},{2,6},{3,7},{4,0},{5,1},{6,2},{7,3},{8,12},{9,13},{10,... | collective-permute-start | bytes 786440 | tf_op jit(solution)/shard_map/ppermute | solution.py:299
  45.0 6.3 %collective-permute-done.7 = bf16[2,512,128]{2,1,0:T(8,128)(2,1)S(1)} collective-permute-done((bf16[2,512,128]{2,1,0:T(8,128)(2,1)S(1)}, bf16[2,512,128]{2,1,0:T(8,128)(2,1)S(1)}, u32[]{:S(2)}, u32[]{:S(2)}) %collective-permute-start.7) | collective-permute-done | bytes 262176 | tf_op jit(solution)/shard_map/ppermute | solution.py:299
  51.3 1.1 collective-permute-start.11
  52.4 0.7 constant_dynamic-update-slice_fusion.7
  53.1 0.7 constant_dynamic-update-slice_fusion.6
  53.8 3.1 %collective-permute-done.8 = bf16[2,512,128]{2,1,0:T(8,128)(2,1)S(1)} collective-permute-done((bf16[2,512,128]{2,1,0:T(8,128)(2,1)S(1)}, bf16[2,512,128]{2,1,0:T(8,128)(2,1)S(1)}, u32[]{:S(2)}, u32[]{:S(2)}) %collective-permute-start.8) | collective-permute-done | bytes 262176 | tf_op jit(solution)/shard_map/ppermute | solution.py:299
  57.0 0.7 constant_dynamic-update-slice_fusion.5.refs_17_
  57.7 0.7 collective-permute-start.13
  58.4 0.3 collective-permute-start.9
  58.8 2.2 %collective-permute-start.15 = (bf16[6,512,128]{2,1,0:T(8,128)(2,1)}, bf16[6,512,128]{2,1,0:T(8,128)(2,1)}, u32[]{:S(2)}, u32[]{:S(2)}) collective-permute-start(bf16[6,512,128]{2,1,0:T(8,128)(2,1)} %constant_dynamic-update-slice_fusion.5.refs_17_), channel_id=1, source_target_pairs={{0,18},{1,19},{2,16},{3,17},{4,22},{5,23},{6,20},{7,21},{8,26},{9,... | collective-permute-start | bytes 2359304 | tf_op jit(solution)/shard_map/ppermute | solution.py:360
  61.0 0.9 collective-permute-start.12
  62.5 45.1 %attend.1.refs_1_.refs_2_.refs_3_.refs_4_.refs_5_.refs_6_.refs_7_.refs_8_.refs_9_.refs_10_.refs_11_.refs_12_.refs_13_.refs_14_.refs_15_.refs_16_.refs_17_.refs_18_ = bf16[64,128,512]{2,1,0:T(8,128)(2,1)} custom-call(s32[17]{0:T(128)S(1)} %convert_reduce_fusion.1.first_ref, s32[128]{0:T(128)S(1)} %get-tuple-element.27.key_ref, s32[2]{0:T(128)S(1)} %pad_add_fusion.me_ref, ...), custom_call_target="tpu_custom_call" | custom-call | flops 1 | bytes 1 | tf_op jit(solution)/shard_map/attend/pallas_call | solution.py:140
  107.6 0.8 copy-done.6
  108.4 6.2 %project.2.refs_25_ = bf16[128,3584]{1,0:T(8,128)(2,1)} custom-call(s32[2]{0:T(128)} %copy-done.2, bf16[128,128]{1,0:T(8,128)(2,1)} %get-tuple-element.29.refs_0_, bf16[64,128,512]{2,1,0:T(8,128)(2,1)} %attend.1.refs_1_.refs_2_.refs_3_.refs_4_.refs_5_.refs_6_.refs_7_.refs_8_.refs_9_.refs_10_.refs_11_.refs_12_.refs_13_.refs_14_.refs_15_.refs_16_.refs_17_.refs_18_, ...), custom_call_target="tpu_custom_call" | custom-call | flops 1 | bytes 1 | tf_op jit(solution)/shard_map/project/pallas_call | solution.py:206
  114.7 0.5 collective-permute-start.17
  115.3 8.2 %index_scores.1 = f32[128,16]{1,0:T(8,128)S(1)} custom-call(s32[2]{0:T(128)S(1)} %copy-done.3, bf16[128,4096]{1,0:T(8,128)(2,1)S(1)} %copy-done, f32[32,128]{1,0:T(8,128)S(1)} %bitcast.21, bf16[4,704,128]{2,1,0:T(8,128)(2,1)S(1)} %bitcast.14, bf16[4,704,128]{2,1,0:T(8,128)(2,1)S(1)} %bitcast.16, bf16[4,704,128]{2,1,0:T(8,128)(2,1)S(1)} %bitcast.18, ...), custom_call_target="tpu_custom_call" | custom-call | flops 1 | bytes 1 | tf_op jit(solution)/shard_map/index_scores/pallas_call | solution.py:275
  123.5 0.7 copy.14
  124.2 7.8 %project.3 = bf16[128,8192]{1,0:T(8,128)(2,1)} custom-call(s32[2]{0:T(128)} %copy-done.2, bf16[128,128]{1,0:T(8,128)(2,1)} %get-tuple-element.29.refs_0_, bf16[64,128,512]{2,1,0:T(8,128)(2,1)} %attend.1.refs_1_.refs_2_.refs_3_.refs_4_.refs_5_.refs_6_.refs_7_.refs_8_.refs_9_.refs_10_.refs_11_.refs_12_.refs_13_.refs_14_.refs_15_.refs_16_.refs_17_.refs_18_, ...), custom_call_target="tpu_custom_call" | custom-call | flops 1 | bytes 1 | tf_op jit(solution)/shard_map/project/pallas_call | solution.py:206
  (44 shorter events, 1.7 us)
Async XLA Ops:
  1.6 12.2 %collective-permute-start = (bf16[704,128]{1,0:T(8,128)(2,1)S(1)}, bf16[704,128]{1,0:T(8,128)(2,1)S(1)}, u32[]{:S(2)}, u32[]{:S(2)}) collective-permute-start(bf16[704,128]{1,0:T(8,128)(2,1)S(1)} %pad_maximum_fusion), channel_id=1, source_target_pairs={{0,8},{1,9},{2,10},{3,11},{4,12},{5,13},{6,14},{7,15},{8,0},{9,1},... | collective-permute-start | bytes 540680 | tf_op jit(solution)/shard_map/ppermute | solution.py:299
  1.7 12.1 %collective-permute-start.1 = (bf16[704,128]{1,0:T(8,128)(2,1)S(1)}, bf16[704,128]{1,0:T(8,128)(2,1)S(1)}, u32[]{:S(2)}, u32[]{:S(2)}) collective-permute-start(bf16[704,128]{1,0:T(8,128)(2,1)S(1)} %pad_maximum_fusion), channel_id=1, source_target_pairs={{0,4},{1,5},{2,6},{3,7},{4,0},{5,1},{6,2},{7,3},{8,12},{9,13},{10,... | collective-permute-start | bytes 540680 | tf_op jit(solution)/shard_map/ppermute | solution.py:299
  2.8 21.8 %collective-permute-start.3 = (bf16[2,512,128]{2,1,0:T(8,128)(2,1)S(1)}, bf16[2,512,128]{2,1,0:T(8,128)(2,1)S(1)}, u32[]{:S(2)}, u32[]{:S(2)}) collective-permute-start(bf16[2,512,128]{2,1,0:T(8,128)(2,1)S(1)} %constant_dynamic-slice_fusion), channel_id=1, source_target_pairs={{0,8},{1,9},{2,10},{3,11},{4,12},{5,13},{6,14},{7,15},{8,0},{9,1},... | collective-permute-start | bytes 786440 | tf_op jit(solution)/shard_map/ppermute | solution.py:299
  13.7 10.9 %collective-permute-start.2 = (bf16[704,128]{1,0:T(8,128)(2,1)S(1)}, bf16[704,128]{1,0:T(8,128)(2,1)S(1)}, u32[]{:S(2)}, u32[]{:S(2)}) collective-permute-start(bf16[704,128]{1,0:T(8,128)(2,1)S(1)} %collective-permute-done), channel_id=1, source_target_pairs={{0,4},{1,5},{2,6},{3,7},{4,0},{5,1},{6,2},{7,3},{8,12},{9,13},{10,... | collective-permute-start | bytes 540680 | tf_op jit(solution)/shard_map/ppermute | solution.py:299
  13.8 29.5 %copy-start.4 = (bf16[4,512,128]{2,1,0:T(8,128)(2,1)S(1)}, bf16[4,512,128]{2,1,0:T(8,128)(2,1)}, u32[]{:S(2)}) copy-start(bf16[4,512,128]{2,1,0:T(8,128)(2,1)} %refs_15_.1) | copy-start | bytes 1572868
  24.7 16.1 %collective-permute-start.4 = (bf16[2816,128]{1,0:T(8,128)(2,1)S(1)}, bf16[2816,128]{1,0:T(8,128)(2,1)S(1)}, u32[]{:S(2)}, u32[]{:S(2)}) collective-permute-start(bf16[2816,128]{1,0:T(8,128)(2,1)S(1)} %constant_dynamic-update-slice_fusion), channel_id=1, source_target_pairs={{0,2},{1,3},{2,0},{3,1},{4,6},{5,7},{6,4},{7,5},{8,10},{9,11},{10,... | collective-permute-start | bytes 2162696 | tf_op jit(solution)/shard_map/ppermute | solution.py:299
  25.0 32.7 %collective-permute-start.5 = (bf16[2816,128]{1,0:T(8,128)(2,1)S(1)}, bf16[2816,128]{1,0:T(8,128)(2,1)S(1)}, u32[]{:S(2)}, u32[]{:S(2)}) collective-permute-start(bf16[2816,128]{1,0:T(8,128)(2,1)S(1)} %constant_dynamic-update-slice_fusion), channel_id=1, source_target_pairs={{0,1},{1,0},{2,3},{3,2},{4,5},{5,4},{6,7},{7,6},{8,9},{9,8},{10,11... | collective-permute-start | bytes 2162696 | tf_op jit(solution)/shard_map/ppermute | solution.py:299
  40.8 16.9 %collective-permute-start.6 = (bf16[2816,128]{1,0:T(8,128)(2,1)S(1)}, bf16[2816,128]{1,0:T(8,128)(2,1)S(1)}, u32[]{:S(2)}, u32[]{:S(2)}) collective-permute-start(bf16[2816,128]{1,0:T(8,128)(2,1)S(1)} %collective-permute-done.4), channel_id=1, source_target_pairs={{0,1},{1,0},{2,3},{3,2},{4,5},{5,4},{6,7},{7,6},{8,9},{9,8},{10,11... | collective-permute-start | bytes 2162696 | tf_op jit(solution)/shard_map/ppermute | solution.py:299
  43.3 8.0 %collective-permute-start.7 = (bf16[2,512,128]{2,1,0:T(8,128)(2,1)S(1)}, bf16[2,512,128]{2,1,0:T(8,128)(2,1)S(1)}, u32[]{:S(2)}, u32[]{:S(2)}) collective-permute-start(bf16[2,512,128]{2,1,0:T(8,128)(2,1)S(1)} %constant_dynamic-slice_fusion), channel_id=1, source_target_pairs={{0,4},{1,5},{2,6},{3,7},{4,0},{5,1},{6,2},{7,3},{8,12},{9,13},{10,... | collective-permute-start | bytes 786440 | tf_op jit(solution)/shard_map/ppermute | solution.py:299
  43.3 15.5 %collective-permute-start.10 = (bf16[4,512,128]{2,1,0:T(8,128)(2,1)S(1)}, bf16[4,512,128]{2,1,0:T(8,128)(2,1)}, u32[]{:S(2)}, u32[]{:S(2)}) collective-permute-start(bf16[4,512,128]{2,1,0:T(8,128)(2,1)S(1)} %copy-done.4), channel_id=1, source_target_pairs={{0,2},{1,3},{2,0},{3,1},{4,6},{5,7},{6,4},{7,5},{8,10},{9,11},{10,... | collective-permute-start | bytes 1572872 | tf_op jit(solution)/shard_map/ppermute | solution.py:299
  43.5 13.4 %collective-permute-start.8 = (bf16[2,512,128]{2,1,0:T(8,128)(2,1)S(1)}, bf16[2,512,128]{2,1,0:T(8,128)(2,1)S(1)}, u32[]{:S(2)}, u32[]{:S(2)}) collective-permute-start(bf16[2,512,128]{2,1,0:T(8,128)(2,1)S(1)} %collective-permute-done.3), channel_id=1, source_target_pairs={{0,4},{1,5},{2,6},{3,7},{4,0},{5,1},{6,2},{7,3},{8,12},{9,13},{10,... | collective-permute-start | bytes 786440 | tf_op jit(solution)/shard_map/ppermute | solution.py:299
  51.3 9.7 %collective-permute-start.11 = (bf16[4,512,128]{2,1,0:T(8,128)(2,1)S(1)}, bf16[4,512,128]{2,1,0:T(8,128)(2,1)S(1)}, u32[]{:S(2)}, u32[]{:S(2)}) collective-permute-start(bf16[4,512,128]{2,1,0:T(8,128)(2,1)S(1)} %copy-done.4), channel_id=1, source_target_pairs={{0,1},{1,0},{2,3},{3,2},{4,5},{5,4},{6,7},{7,6},{8,9},{9,8},{10,11... | collective-permute-start | bytes 1572872 | tf_op jit(solution)/shard_map/ppermute | solution.py:299
  57.7 49.9 %collective-permute-start.13 = (bf16[6,512,128]{2,1,0:T(8,128)(2,1)}, bf16[6,512,128]{2,1,0:T(8,128)(2,1)}, u32[]{:S(2)}, u32[]{:S(2)}) collective-permute-start(bf16[6,512,128]{2,1,0:T(8,128)(2,1)} %constant_dynamic-update-slice_fusion.5.refs_17_), channel_id=1, source_target_pairs={{0,1},{1,0},{2,3},{3,2},{4,5},{5,4},{6,7},{7,6},{8,9},{9,8},{10,11... | collective-permute-start | bytes 2359304 | tf_op jit(solution)/shard_map/ppermute | solution.py:299
  58.4 56.2 %collective-permute-start.9 = (bf16[6,512,128]{2,1,0:T(8,128)(2,1)}, bf16[6,512,128]{2,1,0:T(8,128)(2,1)}, u32[]{:S(2)}, u32[]{:S(2)}) collective-permute-start(bf16[6,512,128]{2,1,0:T(8,128)(2,1)} %constant_dynamic-update-slice_fusion.5.refs_17_), channel_id=1, source_target_pairs={{0,16},{16,0},{1,17},{17,1},{2,18},{18,2},{3,19},{19,3},{4,20},{20... | collective-permute-start | bytes 2359304 | tf_op jit(solution)/shard_map/ppermute | solution.py:358
  58.6 56.0 %collective-permute-start.14 = (bf16[6,512,128]{2,1,0:T(8,128)(2,1)}, bf16[6,512,128]{2,1,0:T(8,128)(2,1)}, u32[]{:S(2)}, u32[]{:S(2)}) collective-permute-start(bf16[6,512,128]{2,1,0:T(8,128)(2,1)} %constant_dynamic-update-slice_fusion.5.refs_17_), channel_id=1, source_target_pairs={{0,2},{1,3},{2,0},{3,1},{4,6},{5,7},{6,4},{7,5},{8,10},{9,11},{10,... | collective-permute-start | bytes 2359304 | tf_op jit(solution)/shard_map/ppermute | solution.py:299
  58.8 55.8 %collective-permute-start.15 = (bf16[6,512,128]{2,1,0:T(8,128)(2,1)}, bf16[6,512,128]{2,1,0:T(8,128)(2,1)}, u32[]{:S(2)}, u32[]{:S(2)}) collective-permute-start(bf16[6,512,128]{2,1,0:T(8,128)(2,1)} %constant_dynamic-update-slice_fusion.5.refs_17_), channel_id=1, source_target_pairs={{0,18},{1,19},{2,16},{3,17},{4,22},{5,23},{6,20},{7,21},{8,26},{9,... | collective-permute-start | bytes 2359304 | tf_op jit(solution)/shard_map/ppermute | solution.py:360
  61.0 1.0 copy-start.5
  61.0 46.6 %collective-permute-start.12 = (bf16[4,512,128]{2,1,0:T(8,128)(2,1)}, bf16[4,512,128]{2,1,0:T(8,128)(2,1)S(1)}, u32[]{:S(2)}, u32[]{:S(2)}) collective-permute-start(bf16[4,512,128]{2,1,0:T(8,128)(2,1)} %collective-permute-done.10.refs_16_), channel_id=1, source_target_pairs={{0,1},{1,0},{2,3},{3,2},{4,5},{5,4},{6,7},{7,6},{8,9},{9,8},{10,11... | collective-permute-start | bytes 1572872 | tf_op jit(solution)/shard_map/ppermute | solution.py:299
  62.4 45.2 %copy-start.2 = (s32[2]{0:T(128)}, s32[2]{0:T(128)S(1)}, u32[]{:S(2)}) copy-start(s32[2]{0:T(128)S(1)} %pad_add_fusion.me_ref) | copy-start | bytes 28
  107.6 0.8 copy-start.6
  108.4 6.9 %copy-start = (bf16[128,4096]{1,0:T(8,128)(2,1)S(1)}, bf16[128,4096]{1,0:T(8,128)(2,1)}, u32[]{:S(2)}) copy-start(bf16[128,4096]{1,0:T(8,128)(2,1)} %q_ref.3) | copy-start | bytes 3145732
  108.4 6.9 %copy-start.1 = (f32[128,32]{0,1:T(8,128)S(1)}, f32[128,32]{0,1:T(8,128)}, u32[]{:S(2)}) copy-start(f32[128,32]{0,1:T(8,128)} %param.11) | copy-start | bytes 49156
  108.4 6.9 %copy-start.3 = (s32[2]{0:T(128)S(1)}, s32[2]{0:T(128)}, u32[]{:S(2)}) copy-start(s32[2]{0:T(128)} %copy-done.2) | copy-start | bytes 28
  114.6 9.6 %collective-permute-start.16 = (bf16[6,512,128]{2,1,0:T(8,128)(2,1)}, bf16[6,512,128]{2,1,0:T(8,128)(2,1)}, u32[]{:S(2)}, u32[]{:S(2)}) collective-permute-start(bf16[6,512,128]{2,1,0:T(8,128)(2,1)} %collective-permute-done.9.refs_19_), channel_id=1, source_target_pairs={{0,1},{1,0},{2,3},{3,2},{4,5},{5,4},{6,7},{7,6},{8,9},{9,8},{10,11... | collective-permute-start | bytes 2359304 | tf_op jit(solution)/shard_map/ppermute | solution.py:299
  114.7 9.5 %collective-permute-start.17 = (bf16[6,512,128]{2,1,0:T(8,128)(2,1)}, bf16[6,512,128]{2,1,0:T(8,128)(2,1)}, u32[]{:S(2)}, u32[]{:S(2)}) collective-permute-start(bf16[6,512,128]{2,1,0:T(8,128)(2,1)} %collective-permute-done.14.refs_20_), channel_id=1, source_target_pairs={{0,1},{1,0},{2,3},{3,2},{4,5},{5,4},{6,7},{7,6},{8,9},{9,8},{10,11... | collective-permute-start | bytes 2359304 | tf_op jit(solution)/shard_map/ppermute | solution.py:299
  115.2 9.0 %collective-permute-start.18 = (bf16[6,512,128]{2,1,0:T(8,128)(2,1)}, bf16[6,512,128]{2,1,0:T(8,128)(2,1)}, u32[]{:S(2)}, u32[]{:S(2)}) collective-permute-start(bf16[6,512,128]{2,1,0:T(8,128)(2,1)} %collective-permute-done.15.refs_21_), channel_id=1, source_target_pairs={{0,1},{1,0},{2,3},{3,2},{4,5},{5,4},{6,7},{7,6},{8,9},{9,8},{10,11... | collective-permute-start | bytes 2359304 | tf_op jit(solution)/shard_map/ppermute | solution.py:299

commit v2 on v1

--- a/solution.py
+++ b/solution.py
@@ -15,7 +15,9 @@
 HI = 32
 DI = 128
 BLK = 128
-WIN = 16
+WIN = 8
+STEP = 32
+AT_ONCE = 2
 DQ = DL + DR
 PACK = DI + DQ
 
@@ -26,12 +28,11 @@
 
 
 def sort_kernel(order_ref, q_ref, out_ref):
-    heads = out_ref.shape[1]
     windows = out_ref.shape[0]
+    heads = out_ref.shape[1] // WIN
     rows = jnp.dot(order_ref[...], q_ref[...], preferred_element_type=f32)
-    for h in range(heads):
-        part = rows[:, h * DQ : (h + 1) * DQ].astype(bf16)
-        out_ref[:, h] = part.reshape(windows, WIN, DQ)
+    parts = [rows[:, h * DQ : (h + 1) * DQ].reshape(windows, WIN, DQ) for h in range(heads)]
+    out_ref[...] = jnp.concatenate(parts, axis=1).astype(bf16)
 
 
 def sort_queries(order, queries):
@@ -44,9 +45,9 @@
             pl.BlockSpec((count, count), lambda i: (0, 0)),
             pl.BlockSpec((count, step * DQ), lambda i: (0, i)),
         ],
-        out_specs=pl.BlockSpec((count // WIN, step, WIN, DQ), lambda i: (0, i, 0, 0)),
-        out_shape=jax.ShapeDtypeStruct((count // WIN, H, WIN, DQ), bf16),
-        compiler_params=pltpu.CompilerParams(vmem_limit_bytes=48 * 2**20),
+        out_specs=pl.BlockSpec((count // WIN, step * WIN, DQ), lambda i: (0, i, 0)),
+        out_shape=jax.ShapeDtypeStruct((count // WIN, H * WIN, DQ), bf16),
+        compiler_params=pltpu.CompilerParams(vmem_limit_bytes=36 * 2**20),
         cost_estimate=SMALL,
         name="sort_queries",
     )(order, queries)
@@ -71,80 +72,99 @@
     return (other & 1) * 8 + ((other >> 1) & 1) * 4 + (other >> 2)
 
 
-def attend_kernel(relative, count, first_ref, key_ref, me_ref, q_ref, pos_ref, keys_ref, *refs):
+def attend_kernel(relative, count, run_ref, offset_ref, key_ref, me_ref, q_ref, pos_ref, keys_ref, *refs):
     pieces = refs[:count]
-    out_ref, rhs_ref = refs[count:]
-    w = pl.program_id(0)
+    out_ref, rhs_ref, acc_ref = refs[count:]
+    step = pl.program_id(0)
     me = me_ref[0]
-    lo = w * WIN
-
-    def load(j, column):
+
+    def load(n, j, column):
         def use(block):
-            rhs_ref[:, column : column + BLK] = block[DI:PACK, :]
+            rhs_ref[n, :, column : column + BLK] = block[DI:PACK, :]
 
         with_block(pieces, place_of(relative, j, me), use)
 
-    @pl.when(w == 0)
+    @pl.when(step == 0)
     def _():
-        load(me, 0)
+        for n in range(AT_ONCE):
+            load(n, me, 0)
 
     column = lax.broadcasted_iota(jnp.int32, (WIN, 2 * BLK), 1)
     last = jnp.where(me > 0, 2 * BLK, 0)
-    usable = (column <= pos_ref[...]) | ((column >= BLK) & (column < last))
-    bias = jnp.where(usable, 0.0, -jnp.inf).astype(f32)
-    keys = keys_ref[...]
-
-    def block(j, carry):
-        start = jnp.maximum(first_ref[j], lo)
-        end = jnp.minimum(first_ref[j + 1], lo + WIN)
-
-        @pl.when(end > start)
-        def _():
-            load(j, BLK)
-            mine = (keys == j)[None]
-            scores = jnp.dot(
-                q_ref[0].reshape(H * WIN, DQ), rhs_ref[...], preferred_element_type=f32
-            ).reshape(H, WIN, 2 * BLK) + bias[None]
+    begin, end = offset_ref[step], offset_ref[step + 1]
+
+    def body(i, carry):
+        windows, rows, weights = [], [], []
+        for n in range(AT_ONCE):
+            token = run_ref[jnp.minimum(begin + i * AT_ONCE + n, end - 1)]
+            j = key_ref[token]
+            load(n, j, BLK)
+            w = token // WIN - step * (STEP // WIN)
+            tokens = pl.ds(pl.multiple_of(w * WIN, WIN), WIN)
+            usable = (column <= pos_ref[tokens]) | ((column >= BLK) & (column < last))
+            windows.append((w, (keys_ref[tokens] == j)[None]))
+            scores = jnp.dot(q_ref[w], rhs_ref[n], preferred_element_type=f32)
+            bias = jnp.where(usable, 0.0, -jnp.inf).astype(f32)
+            rows.append(scores.reshape(H, WIN, 2 * BLK) + bias[None])
+        for scores in rows:
             top = jnp.max(scores, axis=-1, keepdims=True)
             expd = jnp.exp2((scores - top) * exponent_scale)
             total = jnp.sum(expd, axis=-1, keepdims=True)
-            weights = (expd * (1.0 / total)).astype(bf16)
-            values = lax.dot_general(
-                weights.reshape(H * WIN, 2 * BLK),
-                rhs_ref[0:DL, :],
-                (((1,), (1,)), ((), ())),
-                preferred_element_type=f32,
-            ).reshape(H, WIN, DL)
-            old = out_ref[...].astype(f32)
-            out_ref[...] = jnp.where(mine, values, old).astype(bf16)
-
+            weights.append((expd * (1.0 / total)).reshape(H * WIN, 2 * BLK).astype(bf16))
+        values = [
+            lax.dot_general(
+                weights[n], rhs_ref[n, 0:DL, :], (((1,), (1,)), ((), ())), preferred_element_type=f32
+            )
+            for n in range(AT_ONCE)
+        ]
+        for n, (w, mine) in enumerate(windows):
+            old = acc_ref[w].reshape(H, WIN, DL)
+            acc_ref[w] = jnp.where(mine, values[n].reshape(H, WIN, DL), old).reshape(H * WIN, DL)
         return carry
 
-    lax.fori_loop(key_ref[lo], key_ref[lo + WIN - 1] + 1, block, 0)
-
-
-def attend(relative, first, sorted_key, me, sorted_q, pieces, sorted_pos):
+    lax.fori_loop(0, (end - begin + AT_ONCE - 1) // AT_ONCE, body, 0)
+    for w in range(0, STEP // WIN, 2):
+        pair = [acc_ref[w + k].reshape(H, WIN, DL) for k in range(2)]
+        out_ref[:, w * WIN : (w + 2) * WIN] = jnp.concatenate(pair, axis=1).astype(bf16)
+
+
+def runs_of(sorted_key):
     count = sorted_key.shape[0]
+    token = jnp.arange(count, dtype=jnp.int32)
+    starts = (token % WIN == 0) | (sorted_key != jnp.roll(sorted_key, 1))
+    upto = jnp.sum((starts[None, :] & (token[None, :] <= token[:, None])).astype(jnp.int32), axis=1)
+    run = jnp.sum((upto[None, :] <= token[:, None]).astype(jnp.int32), axis=1)
+    first_token = STEP * jnp.arange(count // STEP + 1, dtype=jnp.int32)
+    offset = jnp.sum((starts[None, :] & (token[None, :] < first_token[:, None])).astype(jnp.int32), axis=1)
+    return run, offset
+
+
+def attend(relative, run, offset, sorted_key, me, sorted_q, pieces, pos_column, key_column):
+    count = sorted_key.shape[0]
+    blocks = sum(p.shape[0] for p in pieces)
     spec = pltpu.PrefetchScalarGridSpec(
-        num_scalar_prefetch=3,
-        grid=(count // WIN,),
+        num_scalar_prefetch=4,
+        grid=(count // STEP,),
         in_specs=[
-            pl.BlockSpec((1, H, WIN, DQ), lambda w, *_: (w, 0, 0, 0)),
-            pl.BlockSpec((WIN, 1), lambda w, *_: (w, 0)),
-            pl.BlockSpec((WIN, 1), lambda w, *_: (w, 0)),
+            pl.BlockSpec((STEP // WIN, H * WIN, DQ), lambda w, *_: (w, 0, 0)),
+            pl.BlockSpec((STEP, 1), lambda w, *_: (w, 0)),
+            pl.BlockSpec((STEP, 1), lambda w, *_: (w, 0)),
         ]
         + [pl.BlockSpec((p.shape[0], PACK, BLK), lambda w, *_: (0, 0, 0)) for p in pieces],
-        out_specs=pl.BlockSpec((H, WIN, DL), lambda w, *_: (0, w, 0)),
-        scratch_shapes=[pltpu.VMEM((DQ, 2 * BLK), bf16)],
+        out_specs=pl.BlockSpec((H, STEP, DL), lambda w, *_: (0, w, 0)),
+        scratch_shapes=[
+            pltpu.VMEM((AT_ONCE, DQ, 2 * BLK), bf16),
+            pltpu.VMEM((STEP // WIN, H * WIN, DL), f32),
+        ],
     )
     return pl.pallas_call(
         functools.partial(attend_kernel, relative, len(pieces)),
         grid_spec=spec,
         out_shape=jax.ShapeDtypeStruct((H, count, DL), bf16),
-        compiler_params=pltpu.CompilerParams(vmem_limit_bytes=48 * 2**20),
+        compiler_params=pltpu.CompilerParams(vmem_limit_bytes=(20 + blocks // 2) * 2**20),
         cost_estimate=SMALL,
         name="attend",
-    )(first, sorted_key, me, sorted_q, sorted_pos[:, None], sorted_key[:, None], *pieces)
+    )(run, offset, sorted_key, me, sorted_q, pos_column, key_column, *pieces)
 
 
 def unit_place(unit, me_ref):
@@ -207,7 +227,7 @@
         functools.partial(project_kernel, tuple(units), sizes, tuple(before_units), final),
         grid_spec=spec,
         out_shape=jax.ShapeDtypeStruct((count, width), bf16),
-        compiler_params=pltpu.CompilerParams(vmem_limit_bytes=56 * 2**20),
+        compiler_params=pltpu.CompilerParams(vmem_limit_bytes=36 * 2**20),
         cost_estimate=SMALL,
         name="project",
     )(*operands)
@@ -249,10 +269,10 @@
 
     lax.fori_loop(0, me, step, 0)
     block(me, row <= col)
-    blocks = out_ref.shape[1]
-    sums = acc_ref[...].T[:, 0:blocks]
-    position = me * BLK + lax.broadcasted_iota(jnp.int32, (rows, blocks), 0)
-    block_first = BLK * lax.broadcasted_iota(jnp.int32, (rows, blocks), 1)
+    blocks = out_ref.shape[0]
+    sums = acc_ref[...]
+    position = me * BLK + lax.broadcasted_iota(jnp.int32, (blocks, rows), 1)
+    block_first = BLK * lax.broadcasted_iota(jnp.int32, (blocks, rows), 0)
     counts = jnp.clip(position - block_first + 1, 1, BLK).astype(f32)
     out_ref[...] = sums * (DI ** (-0.5)) / counts
 
@@ -260,7 +280,6 @@
 def index_scores(relative, me, idx_queries, weights_t, pieces):
     count = idx_queries.shape[0]
     blocks = sum(p.shape[0] for p in pieces)
-    rows = -(-blocks // 128) * 128
     spec = pltpu.PrefetchScalarGridSpec(
         num_scalar_prefetch=1,
         grid=(1,),
@@ -269,17 +288,17 @@
             pl.BlockSpec((HI, count), lambda i, *_: (0, 0)),
         ]
         + [pl.BlockSpec((p.shape[0], BLK, DI), lambda i, *_: (0, 0, 0)) for p in pieces],
-        out_specs=pl.BlockSpec((count, blocks), lambda i, *_: (0, 0)),
-        scratch_shapes=[pltpu.VMEM((rows, count), f32), pltpu.VMEM((BLK, DI), bf16)],
+        out_specs=pl.BlockSpec((blocks, count), lambda i, *_: (0, 0)),
+        scratch_shapes=[pltpu.VMEM((blocks, count), f32), pltpu.VMEM((BLK, DI), bf16)],
     )
     return pl.pallas_call(
         functools.partial(index_kernel, relative, len(pieces)),
         grid_spec=spec,
-        out_shape=jax.ShapeDtypeStruct((count, blocks), f32),
-        compiler_params=pltpu.CompilerParams(vmem_limit_bytes=48 * 2**20),
+        out_shape=jax.ShapeDtypeStruct((blocks, count), f32),
+        compiler_params=pltpu.CompilerParams(vmem_limit_bytes=(12 + blocks // 8) * 2**20),
         cost_estimate=SMALL,
         name="index_scores",
-    )(me, idx_queries, weights_t, *pieces)
+    )(me, idx_queries, weights_t, *pieces).T
 
 
 def on_ctx(me_to, devices=16):
@@ -330,19 +349,20 @@
     back = order.T.astype(bf16)
     sorted_key = jnp.sum(jnp.where(order, key[None, :], 0), axis=1)
     sorted_pos = jnp.sum(jnp.where(order, token[None, :], 0), axis=1)
-    first = jnp.sum(
-        (key[None, :] < jnp.arange(blocks + 1, dtype=jnp.int32)[:, None]).astype(jnp.int32), axis=1
-    )
+    run, offset = runs_of(sorted_key)
+    pos_column, key_column = sorted_pos[:, None], sorted_key[:, None]
     order = order.astype(bf16)
     if relative:
-        order = after(order, pack_2)
+        columns = (pos_column, key_column)
+        order, run, offset, meta, columns, _ = lax.optimization_barrier((order, run, offset, meta, columns, pack_2))
+        pos_column, key_column = columns
     sorted_q = sort_queries(order, queries)
 
     if not relative:
         cache = lax.all_gather(pack, "ctx", axis=0, tiled=True).reshape(blocks, PACK, BLK)
         maps = lax.all_gather(value_maps, "ctx", axis=0, tiled=True)
         scores = index_scores(False, meta, idx_queries, idx_weights.T, [cache])
-        latents = attend(False, first, sorted_key, meta, sorted_q, [cache], sorted_pos)
+        latents = attend(False, run, offset, sorted_key, meta, sorted_q, [cache], pos_column, key_column)
         meta = jnp.zeros_like(meta)
         parts = []
         for h in range(0, H, 16):
@@ -352,17 +372,20 @@
 
     half_3 = along(half_2, over_z(1))
     quarter_parts = [half_1, half_2, half_3]
-    column = after(jnp.concatenate(column_parts, axis=0), sorted_q, half_2)
+    column = after(jnp.concatenate(column_parts, axis=0), sorted_q, half_1, half_2, from_y, run, offset, meta, columns)
     column_y = along(column, OVER_Y)
     quarter = jnp.concatenate(quarter_parts, axis=0)
     quarter_x = lax.ppermute(quarter, "groups", [(0, 1), (1, 0)])
     quarter_y = along(quarter, OVER_Y)
     quarter_xy = lax.ppermute(quarter, ("groups", "ctx"), OVER_XY)
-    pieces = [column, column_y, along(column, OVER_CORE), along(column_y, OVER_CORE)]
+    pieces = [column, column_y, along(column, OVER_CORE), along(after(column_y, half_3), OVER_CORE)]
     pieces = [p.reshape(4, PACK, BLK) for p in pieces]
     pieces, quarter = lax.optimization_barrier((pieces, quarter))
 
-    latents = attend(True, first, sorted_key, meta, sorted_q, pieces, sorted_pos)
+    latents = attend(True, run, offset, sorted_key, meta, sorted_q, pieces, pos_column, key_column)
+    latents, quarter_x, quarter_y, quarter_xy = lax.optimization_barrier(
+        (latents, quarter_x, quarter_y, quarter_xy)
+    )
     scores = index_scores(True, meta, idx_queries, idx_weights.T, pieces)
 
     def both_cores(arrays, units):
@@ -374,7 +397,7 @@
         [(0, 0, False), (0, 1, False), (2, 0, False), (2, 1, False)] + [(4 * z, 0, True) for z in (1, 2, 3)],
     )
     early_out = project(meta, back, latents, early_units, early)
-    late_in = [after(a, early_out) for a in (quarter_x, quarter_y, quarter_xy)]
+    late_in = [quarter_x, quarter_y, quarter_xy]
     late, late_units = both_cores(
         late_in,
         [(4 * z, 1, True) for z in (1, 2, 3)]

time: 132 us -> 104 us (0.79)
  Pallas kernels: 76.6 us -> 51.2 us
  waiting for transfers between devices: 30.4 us -> 12 us
  local copies, waits for them, and re-layouts: 6.61 us -> 14.9 us
  starting transfers between devices: 14.9 us -> 21.4 us
    ppermute x17, waiting for transfers between devices: 30.4 us -> 12 us  [along(): return lax.ppermute(array, 'ctx', pairs)]
    pallas_call x1, Pallas kernels: 45.1 us -> 27.5 us  [attend(): pl.pallas_call(functools.partial(attend_kernel, relative, len(pieces)), g...]
    ppermute x17, starting transfers between devices: 12.5 us -> 20.2 us  [along(): return lax.ppermute(array, 'ctx', pairs)]
    unnamed x21 -> x18, local copies, waits for them, and re-layouts: 4.67 us -> 11.7 us
    pallas_call x2, Pallas kernels: 14 us -> 8.75 us  [project(): pl.pallas_call(functools.partial(project_kernel, tuple(units), sizes, tup...]
    pallas_call x1, Pallas kernels: 9.29 us -> 6.16 us  [sort_queries(): pl.pallas_call(sort_kernel, grid=(H // step,), in_specs=[pl.BlockSpec((co...]
  transfers between devices with their start and end apart: 19 -> 19, of which waited for: 5 -> 5; matrix products, arithmetic and copies ran while one was open for 6% -> 8% of each run, Pallas kernels for 52% -> 44%
where the time goes in v2:
time: 104 us; the launch traced here: 103 us
  Pallas kernels  51.2 us (49%)
  starting transfers between devices  21.4 us (21%)
  local copies, waits for them, and re-layouts  14.9 us (14%)
  waiting for transfers between devices  12 us (12%)
  other arithmetic  3.09 us (3%)
    pallas_call x1, Pallas kernels, attend(): pl.pallas_call(functools.partial(attend_kernel, relative, len(pieces)), g...  27.5 us
    ppermute x17, starting transfers between devices, along(): return lax.ppermute(array, 'ctx', pairs)  20.2 us
    ppermute x17, waiting for transfers between devices, along(): return lax.ppermute(array, 'ctx', pairs)  12 us
    unnamed x18, local copies, waits for them, and re-layouts  11.7 us
    pallas_call x1, Pallas kernels, index_scores(): pl.pallas_call(functools.partial(index_kernel, relative, len(pieces)), gr...  8.76 us
    pallas_call x2, Pallas kernels, project(): pl.pallas_call(functools.partial(project_kernel, tuple(units), sizes, tup...  8.75 us
    pallas_call x1, Pallas kernels, sort_queries(): pl.pallas_call(sort_kernel, grid=(H // step,), in_specs=[pl.BlockSpec((co...  6.16 us
  transfers between devices with their start and end apart: 19, of which 5 were waited for; matrix products, arithmetic and copies ran while one was open for 8% of the time, Pallas kernels for 44%

profile of v2, /device:TPU:31, one launch (start us, length us, event | category | flops | bytes accessed | tf_op | source)
XLA Modules:
  0.0 103.3 jit_solution(16147637770580632230)
XLA Ops:
  0.6 0.9 pad_maximum_fusion
  1.9 1.0 constant_dynamic-slice_fusion
  2.8 1.4 %collective-permute-start.3 = (bf16[2,512,128]{2,1,0:T(8,128)(2,1)S(1)}, bf16[2,512,128]{2,1,0:T(8,128)(2,1)S(1)}, u32[]{:S(2)}, u32[]{:S(2)}) collective-permute-start(bf16[2,512,128]{2,1,0:T(8,128)(2,1)S(1)} %constant_dynamic-slice_fusion), channel_id=1, source_target_pairs={{0,4},{1,5},{2,6},{3,7},{4,0},{5,1},{6,2},{7,3},{8,12},{9,13},{10,... | collective-permute-start | bytes 786440 | tf_op jit(solution)/shard_map/ppermute | solution.py:318
  4.2 2.3 %collective-permute-start.4 = (bf16[2,512,128]{2,1,0:T(8,128)(2,1)S(1)}, bf16[2,512,128]{2,1,0:T(8,128)(2,1)S(1)}, u32[]{:S(2)}, u32[]{:S(2)}) collective-permute-start(bf16[2,512,128]{2,1,0:T(8,128)(2,1)S(1)} %constant_dynamic-slice_fusion), channel_id=1, source_target_pairs={{0,8},{1,9},{2,10},{3,11},{4,12},{5,13},{6,14},{7,15},{8,0},{9,1},... | collective-permute-start | bytes 786440 | tf_op jit(solution)/shard_map/ppermute | solution.py:318
  6.7 0.8 constant_dynamic-update-slice_fusion.4
  7.5 0.7 fusion.6
  8.4 0.6 slice.12
  9.0 0.7 compare_or_fusion
  10.1 0.9 constant_dynamic-update-slice_fusion.3
  11.3 1.5 %collective-permute-done = bf16[704,128]{1,0:T(8,128)(2,1)S(1)} collective-permute-done((bf16[704,128]{1,0:T(8,128)(2,1)S(1)}, bf16[704,128]{1,0:T(8,128)(2,1)S(1)}, u32[]{:S(2)}, u32[]{:S(2)}) %collective-permute-start) | collective-permute-done | bytes 180256 | tf_op jit(solution)/shard_map/ppermute | solution.py:318
  12.8 3.7 %copy-done.1 = bf16[128,36864]{1,0:T(8,128)(2,1)S(1)} copy-done((bf16[128,36864]{1,0:T(8,128)(2,1)S(1)}, bf16[128,36864]{1,0:T(8,128)(2,1)}, u32[]{:S(2)}) %copy-start.1) | copy-done | bytes 9437208
  16.5 6.2 %sort_queries.1.q_ref = bf16[16,512,576]{2,1,0:T(8,128)(2,1)} custom-call(bf16[128,128]{1,0:T(8,128)(2,1)S(1)} %get-tuple-element.22.order_ref, bf16[128,36864]{1,0:T(8,128)(2,1)S(1)} %copy-done.1), custom_call_target="tpu_custom_call" | custom-call | flops 1 | bytes 1 | tf_op jit(solution)/shard_map/sort_queries/pallas_call | solution.py:41
  22.7 3.1 %collective-permute-done.2 = bf16[704,128]{1,0:T(8,128)(2,1)S(1)} collective-permute-done((bf16[704,128]{1,0:T(8,128)(2,1)S(1)}, bf16[704,128]{1,0:T(8,128)(2,1)S(1)}, u32[]{:S(2)}, u32[]{:S(2)}) %collective-permute-start.2) | collective-permute-done | bytes 180256 | tf_op jit(solution)/shard_map/ppermute | solution.py:318
  26.5 0.7 constant_dynamic-update-slice_fusion.7
  27.2 3.1 %collective-permute-start.7 = (bf16[2816,128]{1,0:T(8,128)(2,1)S(1)}, bf16[2816,128]{1,0:T(8,128)(2,1)S(1)}, u32[]{:S(2)}, u32[]{:S(2)}) collective-permute-start(bf16[2816,128]{1,0:T(8,128)(2,1)S(1)} %constant_dynamic-update-slice_fusion), channel_id=1, source_target_pairs={{0,1},{1,0},{2,3},{3,2},{4,5},{5,4},{6,7},{7,6},{8,9},{9,8},{10,11... | collective-permute-start | bytes 2162696 | tf_op jit(solution)/shard_map/ppermute | solution.py:318
  30.3 0.7 constant_dynamic-update-slice_fusion.6
  31.4 0.7 constant_dynamic-update-slice_fusion.5.refs_17_
  32.4 1.5 %collective-permute-start.11 = (bf16[6,512,128]{2,1,0:T(8,128)(2,1)}, bf16[6,512,128]{2,1,0:T(8,128)(2,1)}, u32[]{:S(2)}, u32[]{:S(2)}) collective-permute-start(bf16[6,512,128]{2,1,0:T(8,128)(2,1)} %constant_dynamic-update-slice_fusion.5.refs_17_), channel_id=1, source_target_pairs={{0,2},{1,3},{2,0},{3,1},{4,6},{5,7},{6,4},{7,5},{8,10},{9,11},{10,... | collective-permute-start | bytes 2359304 | tf_op jit(solution)/shard_map/ppermute | solution.py:318
  33.9 0.9 collective-permute-start.12
  34.9 5.7 %collective-permute-done.6 = bf16[2816,128]{1,0:T(8,128)(2,1)S(1)} collective-permute-done((bf16[2816,128]{1,0:T(8,128)(2,1)S(1)}, bf16[2816,128]{1,0:T(8,128)(2,1)S(1)}, u32[]{:S(2)}, u32[]{:S(2)}) %collective-permute-start.6) | collective-permute-done | bytes 720928 | tf_op jit(solution)/shard_map/ppermute | solution.py:318
  40.6 7.6 %collective-permute-start.9 = (bf16[2816,128]{1,0:T(8,128)(2,1)S(1)}, bf16[2816,128]{1,0:T(8,128)(2,1)S(1)}, u32[]{:S(2)}, u32[]{:S(2)}) collective-permute-start(bf16[2816,128]{1,0:T(8,128)(2,1)S(1)} %collective-permute-done.6), channel_id=1, source_target_pairs={{0,1},{1,0},{2,3},{3,2},{4,5},{5,4},{6,7},{7,6},{8,9},{9,8},{10,11... | collective-permute-start | bytes 2162696 | tf_op jit(solution)/shard_map/ppermute | solution.py:318
  48.3 0.7 copy.12.keys_ref
  49.1 1.2 %collective-permute-done.9 = bf16[2816,128]{1,0:T(8,128)(2,1)S(1)} collective-permute-done((bf16[2816,128]{1,0:T(8,128)(2,1)S(1)}, bf16[2816,128]{1,0:T(8,128)(2,1)S(1)}, u32[]{:S(2)}, u32[]{:S(2)}) %collective-permute-start.9) | collective-permute-done | bytes 720928 | tf_op jit(solution)/shard_map/ppermute | solution.py:318
  50.2 4.0 %copy-done = bf16[16,512,576]{2,1,0:T(8,128)(2,1)S(1)} copy-done((bf16[16,512,576]{2,1,0:T(8,128)(2,1)S(1)}, bf16[16,512,576]{2,1,0:T(8,128)(2,1)}, u32[]{:S(2)}) %copy-start) | copy-done | bytes 9437208
  54.2 0.8 copy-done.4
  55.0 27.5 %attend.1.refs_1_.refs_2_.refs_3_.refs_4_.refs_5_.refs_6_.refs_7_.refs_8_.refs_9_.refs_10_.refs_11_.refs_12_.refs_13_.refs_14_.refs_15_.refs_16_.refs_17_.refs_18_ = bf16[64,128,512]{2,1,0:T(8,128)(2,1)S(1)} custom-call(s32[128]{0:T(128)S(1)} %convert_reduce_fusion.run_ref, s32[5]{0:T(128)S(1)} %convert_reduce_fusion.3.offset_ref, ...), custom_call_target="tpu_custom_call" | custom-call | flops 1 | bytes 1 | tf_op jit(solution)/shard_map/attend/pallas_call | solution.py:160
  82.6 2.1 %collective-permute-start.18 = (bf16[6,512,128]{2,1,0:T(8,128)(2,1)}, bf16[6,512,128]{2,1,0:T(8,128)(2,1)S(1)}, u32[]{:S(2)}, u32[]{:S(2)}) collective-permute-start(bf16[6,512,128]{2,1,0:T(8,128)(2,1)} %constant_dynamic-update-slice_fusion.5.refs_17_), channel_id=1, source_target_pairs={{0,1},{1,0},{2,3},{3,2},{4,5},{5,4},{6,7},{7,6},{8,9},{9,8},{10,11... | collective-permute-start | bytes 2359304 | tf_op jit(solution)/shard_map/ppermute | solution.py:318
  84.8 0.4 collective-permute-start.14
  85.3 0.4 collective-permute-start.17
  85.8 8.8 %index_scores.1 = f32[16,128]{1,0:T(8,128)} custom-call(s32[2]{0:T(128)S(1)} %pad_add_fusion.me_ref, bf16[128,4096]{1,0:T(8,128)(2,1)S(1)} %copy-done.3, f32[32,128]{1,0:T(8,128)S(1)} %bitcast.23, bf16[4,704,128]{2,1,0:T(8,128)(2,1)S(1)} %bitcast.16, bf16[4,704,128]{2,1,0:T(8,128)(2,1)S(1)} %bitcast.18, bf16[4,704,128]{2,1,0:T(8,128)(2,1)S(1)} %bitcast.20, ...), custom_call_target="tpu_custom_call" | custom-call | flops 1 | bytes 1 | tf_op jit(solution)/shard_map/index_scores/pallas_call | solution.py:294
  94.5 3.4 %project.2.refs_25_ = bf16[128,3584]{1,0:T(8,128)(2,1)S(1)} custom-call(s32[2]{0:T(128)S(1)} %pad_add_fusion.me_ref, bf16[128,128]{1,0:T(8,128)(2,1)S(1)} %get-tuple-element.38.refs_0_, ...), custom_call_target="tpu_custom_call" | custom-call | flops 1 | bytes 1 | tf_op jit(solution)/shard_map/project/pallas_call | solution.py:226
  97.9 5.4 %project.3 = bf16[128,8192]{1,0:T(8,128)(2,1)} custom-call(s32[2]{0:T(128)S(1)} %pad_add_fusion.me_ref, bf16[128,128]{1,0:T(8,128)(2,1)S(1)} %get-tuple-element.38.refs_0_, ...), custom_call_target="tpu_custom_call" | custom-call | flops 1 | bytes 1 | tf_op jit(solution)/shard_map/project/pallas_call | solution.py:226
  (46 shorter events, 3.0 us)
Async XLA Ops:
  1.6 11.2 %collective-permute-start = (bf16[704,128]{1,0:T(8,128)(2,1)S(1)}, bf16[704,128]{1,0:T(8,128)(2,1)S(1)}, u32[]{:S(2)}, u32[]{:S(2)}) collective-permute-start(bf16[704,128]{1,0:T(8,128)(2,1)S(1)} %pad_maximum_fusion), channel_id=1, source_target_pairs={{0,8},{1,9},{2,10},{3,11},{4,12},{5,13},{6,14},{7,15},{8,0},{9,1},... | collective-permute-start | bytes 540680 | tf_op jit(solution)/shard_map/ppermute | solution.py:318
  1.7 11.1 %collective-permute-start.1 = (bf16[704,128]{1,0:T(8,128)(2,1)S(1)}, bf16[704,128]{1,0:T(8,128)(2,1)S(1)}, u32[]{:S(2)}, u32[]{:S(2)}) collective-permute-start(bf16[704,128]{1,0:T(8,128)(2,1)S(1)} %pad_maximum_fusion), channel_id=1, source_target_pairs={{0,4},{1,5},{2,6},{3,7},{4,0},{5,1},{6,2},{7,3},{8,12},{9,13},{10,... | collective-permute-start | bytes 540680 | tf_op jit(solution)/shard_map/ppermute | solution.py:318
  2.8 23.0 %collective-permute-start.3 = (bf16[2,512,128]{2,1,0:T(8,128)(2,1)S(1)}, bf16[2,512,128]{2,1,0:T(8,128)(2,1)S(1)}, u32[]{:S(2)}, u32[]{:S(2)}) collective-permute-start(bf16[2,512,128]{2,1,0:T(8,128)(2,1)S(1)} %constant_dynamic-slice_fusion), channel_id=1, source_target_pairs={{0,4},{1,5},{2,6},{3,7},{4,0},{5,1},{6,2},{7,3},{8,12},{9,13},{10,... | collective-permute-start | bytes 786440 | tf_op jit(solution)/shard_map/ppermute | solution.py:318
  4.2 21.7 %collective-permute-start.4 = (bf16[2,512,128]{2,1,0:T(8,128)(2,1)S(1)}, bf16[2,512,128]{2,1,0:T(8,128)(2,1)S(1)}, u32[]{:S(2)}, u32[]{:S(2)}) collective-permute-start(bf16[2,512,128]{2,1,0:T(8,128)(2,1)S(1)} %constant_dynamic-slice_fusion), channel_id=1, source_target_pairs={{0,8},{1,9},{2,10},{3,11},{4,12},{5,13},{6,14},{7,15},{8,0},{9,1},... | collective-permute-start | bytes 786440 | tf_op jit(solution)/shard_map/ppermute | solution.py:318
  6.5 19.4 %collective-permute-start.5 = (bf16[4,512,128]{2,1,0:T(8,128)(2,1)}, bf16[4,512,128]{2,1,0:T(8,128)(2,1)}, u32[]{:S(2)}, u32[]{:S(2)}) collective-permute-start(bf16[4,512,128]{2,1,0:T(8,128)(2,1)} %refs_15_.1), channel_id=1, source_target_pairs={{0,2},{1,3},{2,0},{3,1},{4,6},{5,7},{6,4},{7,5},{8,10},{9,11},{10,... | collective-permute-start | bytes 1572872 | tf_op jit(solution)/shard_map/ppermute | solution.py:318
  12.8 13.1 %collective-permute-start.2 = (bf16[704,128]{1,0:T(8,128)(2,1)S(1)}, bf16[704,128]{1,0:T(8,128)(2,1)S(1)}, u32[]{:S(2)}, u32[]{:S(2)}) collective-permute-start(bf16[704,128]{1,0:T(8,128)(2,1)S(1)} %collective-permute-done), channel_id=1, source_target_pairs={{0,4},{1,5},{2,6},{3,7},{4,0},{5,1},{6,2},{7,3},{8,12},{9,13},{10,... | collective-permute-start | bytes 540680 | tf_op jit(solution)/shard_map/ppermute | solution.py:318
  12.8 3.7 %copy-start.1 = (bf16[128,36864]{1,0:T(8,128)(2,1)S(1)}, bf16[128,36864]{1,0:T(8,128)(2,1)}, u32[]{:S(2)}) copy-start(bf16[128,36864]{1,0:T(8,128)(2,1)} %q_ref.2) | copy-start | bytes 28311556
  16.5 31.6 %copy-start.2 = (bf16[4,512,128]{2,1,0:T(8,128)(2,1)S(1)}, bf16[4,512,128]{2,1,0:T(8,128)(2,1)}, u32[]{:S(2)}) copy-start(bf16[4,512,128]{2,1,0:T(8,128)(2,1)} %refs_15_.1) | copy-start | bytes 1572868
  25.9 14.7 %collective-permute-start.6 = (bf16[2816,128]{1,0:T(8,128)(2,1)S(1)}, bf16[2816,128]{1,0:T(8,128)(2,1)S(1)}, u32[]{:S(2)}, u32[]{:S(2)}) collective-permute-start(bf16[2816,128]{1,0:T(8,128)(2,1)S(1)} %constant_dynamic-update-slice_fusion), channel_id=1, source_target_pairs={{0,2},{1,3},{2,0},{3,1},{4,6},{5,7},{6,4},{7,5},{8,10},{9,11},{10,... | collective-permute-start | bytes 2162696 | tf_op jit(solution)/shard_map/ppermute | solution.py:318
  26.2 5.2 %collective-permute-start.8 = (bf16[2,512,128]{2,1,0:T(8,128)(2,1)S(1)}, bf16[2,512,128]{2,1,0:T(8,128)(2,1)S(1)}, u32[]{:S(2)}, u32[]{:S(2)}) collective-permute-start(bf16[2,512,128]{2,1,0:T(8,128)(2,1)S(1)} %collective-permute-done.4), channel_id=1, source_target_pairs={{0,4},{1,5},{2,6},{3,7},{4,0},{5,1},{6,2},{7,3},{8,12},{9,13},{10,... | collective-permute-start | bytes 786440 | tf_op jit(solution)/shard_map/ppermute | solution.py:318
  27.2 20.9 %collective-permute-start.7 = (bf16[2816,128]{1,0:T(8,128)(2,1)S(1)}, bf16[2816,128]{1,0:T(8,128)(2,1)S(1)}, u32[]{:S(2)}, u32[]{:S(2)}) collective-permute-start(bf16[2816,128]{1,0:T(8,128)(2,1)S(1)} %constant_dynamic-update-slice_fusion), channel_id=1, source_target_pairs={{0,1},{1,0},{2,3},{3,2},{4,5},{5,4},{6,7},{7,6},{8,9},{9,8},{10,11... | collective-permute-start | bytes 2162696 | tf_op jit(solution)/shard_map/ppermute | solution.py:318
  32.1 50.4 %collective-permute-start.10 = (bf16[6,512,128]{2,1,0:T(8,128)(2,1)}, bf16[6,512,128]{2,1,0:T(8,128)(2,1)}, u32[]{:S(2)}, u32[]{:S(2)}) collective-permute-start(bf16[6,512,128]{2,1,0:T(8,128)(2,1)} %constant_dynamic-update-slice_fusion.5.refs_17_), channel_id=1, source_target_pairs={{0,16},{16,0},{1,17},{17,1},{2,18},{18,2},{3,19},{19,3},{4,20},{20... | collective-permute-start | bytes 2359304 | tf_op jit(solution)/shard_map/ppermute | solution.py:378
  32.4 50.2 %collective-permute-start.11 = (bf16[6,512,128]{2,1,0:T(8,128)(2,1)}, bf16[6,512,128]{2,1,0:T(8,128)(2,1)}, u32[]{:S(2)}, u32[]{:S(2)}) collective-permute-start(bf16[6,512,128]{2,1,0:T(8,128)(2,1)} %constant_dynamic-update-slice_fusion.5.refs_17_), channel_id=1, source_target_pairs={{0,2},{1,3},{2,0},{3,1},{4,6},{5,7},{6,4},{7,5},{8,10},{9,11},{10,... | collective-permute-start | bytes 2359304 | tf_op jit(solution)/shard_map/ppermute | solution.py:318
  33.9 48.7 %collective-permute-start.12 = (bf16[6,512,128]{2,1,0:T(8,128)(2,1)}, bf16[6,512,128]{2,1,0:T(8,128)(2,1)}, u32[]{:S(2)}, u32[]{:S(2)}) collective-permute-start(bf16[6,512,128]{2,1,0:T(8,128)(2,1)} %constant_dynamic-update-slice_fusion.5.refs_17_), channel_id=1, source_target_pairs={{0,18},{1,19},{2,16},{3,17},{4,22},{5,23},{6,20},{7,21},{8,26},{9,... | collective-permute-start | bytes 2359304 | tf_op jit(solution)/shard_map/ppermute | solution.py:380
  40.6 9.6 %collective-permute-start.9 = (bf16[2816,128]{1,0:T(8,128)(2,1)S(1)}, bf16[2816,128]{1,0:T(8,128)(2,1)S(1)}, u32[]{:S(2)}, u32[]{:S(2)}) collective-permute-start(bf16[2816,128]{1,0:T(8,128)(2,1)S(1)} %collective-permute-done.6), channel_id=1, source_target_pairs={{0,1},{1,0},{2,3},{3,2},{4,5},{5,4},{6,7},{7,6},{8,9},{9,8},{10,11... | collective-permute-start | bytes 2162696 | tf_op jit(solution)/shard_map/ppermute | solution.py:318
  48.2 37.2 %collective-permute-start.16 = (bf16[4,512,128]{2,1,0:T(8,128)(2,1)S(1)}, bf16[4,512,128]{2,1,0:T(8,128)(2,1)}, u32[]{:S(2)}, u32[]{:S(2)}) collective-permute-start(bf16[4,512,128]{2,1,0:T(8,128)(2,1)S(1)} %copy-done.2), channel_id=1, source_target_pairs={{0,1},{1,0},{2,3},{3,2},{4,5},{5,4},{6,7},{7,6},{8,9},{9,8},{10,11... | collective-permute-start | bytes 1572872 | tf_op jit(solution)/shard_map/ppermute | solution.py:318
  50.2 4.0 %copy-start = (bf16[16,512,576]{2,1,0:T(8,128)(2,1)S(1)}, bf16[16,512,576]{2,1,0:T(8,128)(2,1)}, u32[]{:S(2)}) copy-start(bf16[16,512,576]{2,1,0:T(8,128)(2,1)} %sort_queries.1.q_ref) | copy-start | bytes 28311556
  54.2 0.8 copy-start.4
  55.0 30.7 %copy-start.3 = (bf16[128,4096]{1,0:T(8,128)(2,1)S(1)}, bf16[128,4096]{1,0:T(8,128)(2,1)}, u32[]{:S(2)}) copy-start(bf16[128,4096]{1,0:T(8,128)(2,1)} %q_ref.3) | copy-start | bytes 3145732
  55.0 30.7 %copy-start.5 = (f32[128,32]{0,1:T(8,128)S(1)}, f32[128,32]{0,1:T(8,128)}, u32[]{:S(2)}) copy-start(f32[128,32]{0,1:T(8,128)} %param.11) | copy-start | bytes 49156
  82.6 11.9 %collective-permute-start.18 = (bf16[6,512,128]{2,1,0:T(8,128)(2,1)}, bf16[6,512,128]{2,1,0:T(8,128)(2,1)S(1)}, u32[]{:S(2)}, u32[]{:S(2)}) collective-permute-start(bf16[6,512,128]{2,1,0:T(8,128)(2,1)} %constant_dynamic-update-slice_fusion.5.refs_17_), channel_id=1, source_target_pairs={{0,1},{1,0},{2,3},{3,2},{4,5},{5,4},{6,7},{7,6},{8,9},{9,8},{10,11... | collective-permute-start | bytes 2359304 | tf_op jit(solution)/shard_map/ppermute | solution.py:318
  84.7 13.2 %collective-permute-start.13 = (bf16[6,512,128]{2,1,0:T(8,128)(2,1)}, bf16[6,512,128]{2,1,0:T(8,128)(2,1)S(1)}, u32[]{:S(2)}, u32[]{:S(2)}) collective-permute-start(bf16[6,512,128]{2,1,0:T(8,128)(2,1)} %collective-permute-done.10.refs_19_), channel_id=1, source_target_pairs={{0,1},{1,0},{2,3},{3,2},{4,5},{5,4},{6,7},{7,6},{8,9},{9,8},{10,11... | collective-permute-start | bytes 2359304 | tf_op jit(solution)/shard_map/ppermute | solution.py:318
  84.8 13.1 %collective-permute-start.14 = (bf16[6,512,128]{2,1,0:T(8,128)(2,1)}, bf16[6,512,128]{2,1,0:T(8,128)(2,1)S(1)}, u32[]{:S(2)}, u32[]{:S(2)}) collective-permute-start(bf16[6,512,128]{2,1,0:T(8,128)(2,1)} %collective-permute-done.11.refs_20_), channel_id=1, source_target_pairs={{0,1},{1,0},{2,3},{3,2},{4,5},{5,4},{6,7},{7,6},{8,9},{9,8},{10,11... | collective-permute-start | bytes 2359304 | tf_op jit(solution)/shard_map/ppermute | solution.py:318
  85.2 12.7 %collective-permute-start.15 = (bf16[6,512,128]{2,1,0:T(8,128)(2,1)}, bf16[6,512,128]{2,1,0:T(8,128)(2,1)S(1)}, u32[]{:S(2)}, u32[]{:S(2)}) collective-permute-start(bf16[6,512,128]{2,1,0:T(8,128)(2,1)} %collective-permute-done.12.refs_21_), channel_id=1, source_target_pairs={{0,1},{1,0},{2,3},{3,2},{4,5},{5,4},{6,7},{7,6},{8,9},{9,8},{10,11... | collective-permute-start | bytes 2359304 | tf_op jit(solution)/shard_map/ppermute | solution.py:318
  85.3 9.2 %collective-permute-start.17 = (bf16[4,512,128]{2,1,0:T(8,128)(2,1)}, bf16[4,512,128]{2,1,0:T(8,128)(2,1)S(1)}, u32[]{:S(2)}, u32[]{:S(2)}) collective-permute-start(bf16[4,512,128]{2,1,0:T(8,128)(2,1)} %collective-permute-done.5.refs_16_), channel_id=1, source_target_pairs={{0,1},{1,0},{2,3},{3,2},{4,5},{5,4},{6,7},{7,6},{8,9},{9,8},{10,11... | collective-permute-start | bytes 1572872 | tf_op jit(solution)/shard_map/ppermute | solution.py:318

commit v3 on v2

--- a/solution.py
+++ b/solution.py
@@ -16,7 +16,7 @@
 DI = 128
 BLK = 128
 WIN = 8
-STEP = 32
+STEP = 64
 AT_ONCE = 2
 DQ = DL + DR
 PACK = DI + DQ
@@ -80,7 +80,7 @@
 
     def load(n, j, column):
         def use(block):
-            rhs_ref[n, :, column : column + BLK] = block[DI:PACK, :]
+            rhs_ref[n, :, column : column + BLK] = block[...]
 
         with_block(pieces, place_of(relative, j, me), use)
 
@@ -101,8 +101,8 @@
             load(n, j, BLK)
             w = token // WIN - step * (STEP // WIN)
             tokens = pl.ds(pl.multiple_of(w * WIN, WIN), WIN)
-            usable = (column <= pos_ref[tokens]) | ((column >= BLK) & (column < last))
-            windows.append((w, (keys_ref[tokens] == j)[None]))
+            usable = (column <= pos_ref[tokens][:, 0:1]) | ((column >= BLK) & (column < last))
+            windows.append((w, (keys_ref[tokens][:, 0:1] == j)[None]))
             scores = jnp.dot(q_ref[w], rhs_ref[n], preferred_element_type=f32)
             bias = jnp.where(usable, 0.0, -jnp.inf).astype(f32)
             rows.append(scores.reshape(H, WIN, 2 * BLK) + bias[None])
@@ -147,10 +147,10 @@
         grid=(count // STEP,),
         in_specs=[
             pl.BlockSpec((STEP // WIN, H * WIN, DQ), lambda w, *_: (w, 0, 0)),
-            pl.BlockSpec((STEP, 1), lambda w, *_: (w, 0)),
-            pl.BlockSpec((STEP, 1), lambda w, *_: (w, 0)),
+            pl.BlockSpec((STEP, BLK), lambda w, *_: (w, 0)),
+            pl.BlockSpec((STEP, BLK), lambda w, *_: (w, 0)),
         ]
-        + [pl.BlockSpec((p.shape[0], PACK, BLK), lambda w, *_: (0, 0, 0)) for p in pieces],
+        + [pl.BlockSpec((p.shape[0], DQ, BLK), lambda w, *_: (0, 0, 0)) for p in pieces],
         out_specs=pl.BlockSpec((H, STEP, DL), lambda w, *_: (0, w, 0)),
         scratch_shapes=[
             pltpu.VMEM((AT_ONCE, DQ, 2 * BLK), bf16),
@@ -161,7 +161,7 @@
         functools.partial(attend_kernel, relative, len(pieces)),
         grid_spec=spec,
         out_shape=jax.ShapeDtypeStruct((H, count, DL), bf16),
-        compiler_params=pltpu.CompilerParams(vmem_limit_bytes=(20 + blocks // 2) * 2**20),
+        compiler_params=pltpu.CompilerParams(vmem_limit_bytes=(30 + blocks // 2) * 2**20),
         cost_estimate=SMALL,
         name="attend",
     )(run, offset, sorted_key, me, sorted_q, pos_column, key_column, *pieces)
@@ -318,6 +318,10 @@
     return lax.ppermute(array, "ctx", pairs)
 
 
+def across(array):
+    return lax.ppermute(array, "groups", [(0, 1), (1, 0)])
+
+
 def after(array, *others):
     return lax.optimization_barrier((array,) + others)[0]
 
@@ -350,19 +354,22 @@
     sorted_key = jnp.sum(jnp.where(order, key[None, :], 0), axis=1)
     sorted_pos = jnp.sum(jnp.where(order, token[None, :], 0), axis=1)
     run, offset = runs_of(sorted_key)
-    pos_column, key_column = sorted_pos[:, None], sorted_key[:, None]
+    pos_column = jnp.broadcast_to(sorted_pos[:, None], (count, BLK))
+    key_column = jnp.broadcast_to(sorted_key[:, None], (count, BLK))
     order = order.astype(bf16)
     if relative:
         columns = (pos_column, key_column)
-        order, run, offset, meta, columns, _ = lax.optimization_barrier((order, run, offset, meta, columns, pack_2))
+        order, run, offset, meta, columns, _, half_2 = lax.optimization_barrier(
+            (order, run, offset, meta, columns, pack_2, half_2)
+        )
         pos_column, key_column = columns
     sorted_q = sort_queries(order, queries)
 
     if not relative:
         cache = lax.all_gather(pack, "ctx", axis=0, tiled=True).reshape(blocks, PACK, BLK)
         maps = lax.all_gather(value_maps, "ctx", axis=0, tiled=True)
-        scores = index_scores(False, meta, idx_queries, idx_weights.T, [cache])
-        latents = attend(False, run, offset, sorted_key, meta, sorted_q, [cache], pos_column, key_column)
+        scores = index_scores(False, meta, idx_queries, idx_weights.T, [cache[:, 0:DI]])
+        latents = attend(False, run, offset, sorted_key, meta, sorted_q, [cache[:, DI:PACK]], pos_column, key_column)
         meta = jnp.zeros_like(meta)
         parts = []
         for h in range(0, H, 16):
@@ -371,40 +378,42 @@
         return (jnp.concatenate(parts, axis=1), scores)
 
     half_3 = along(half_2, over_z(1))
-    quarter_parts = [half_1, half_2, half_3]
-    column = after(jnp.concatenate(column_parts, axis=0), sorted_q, half_1, half_2, from_y, run, offset, meta, columns)
+    first = jnp.concatenate([half_1, half_2], axis=0)
+    first_x, first_y = across(first), along(first, OVER_Y)
+    early_keys = jnp.concatenate([p[0:DI] for p in column_parts], axis=0)
+    keys_y = along(early_keys, OVER_Y)
+    keys_plane = jnp.concatenate([early_keys, keys_y], axis=0)
+    keys = [keys_plane, along(keys_plane, OVER_CORE)]
+    keys = [p.reshape(8, BLK, DI) for p in keys]
+    scores = index_scores(True, meta, idx_queries, idx_weights.T, keys)
+    column = jnp.concatenate([p[DI:PACK] for p in column_parts], axis=0)
+    column = after(column, sorted_q, first_x, first_y, half_3, from_y, run, offset, meta, columns)
     column_y = along(column, OVER_Y)
-    quarter = jnp.concatenate(quarter_parts, axis=0)
-    quarter_x = lax.ppermute(quarter, "groups", [(0, 1), (1, 0)])
-    quarter_y = along(quarter, OVER_Y)
-    quarter_xy = lax.ppermute(quarter, ("groups", "ctx"), OVER_XY)
-    pieces = [column, column_y, along(column, OVER_CORE), along(after(column_y, half_3), OVER_CORE)]
-    pieces = [p.reshape(4, PACK, BLK) for p in pieces]
-    pieces, quarter = lax.optimization_barrier((pieces, quarter))
+    last_y = along(half_3, OVER_Y)
+    from_x = across(jnp.concatenate([first_y, half_3], axis=0))
+    last_xy = lax.ppermute(half_3, ("groups", "ctx"), OVER_XY)
+    early = [value_maps, from_y, first, half_3]
+    early_core = [along(a, OVER_CORE) for a in early]
+    pieces = [column, column_y, along(column, OVER_CORE), along(after(column_y, scores, early_core), OVER_CORE)]
+    pieces = [p.reshape(4, DQ, BLK) for p in pieces]
+    first_core = [along(first_x, OVER_CORE), along(first_y, OVER_CORE)]
 
     latents = attend(True, run, offset, sorted_key, meta, sorted_q, pieces, pos_column, key_column)
-    latents, quarter_x, quarter_y, quarter_xy = lax.optimization_barrier(
-        (latents, quarter_x, quarter_y, quarter_xy)
+    latents, first_core, from_x, last_y, last_xy = lax.optimization_barrier(
+        (latents, first_core, from_x, last_y, last_xy)
     )
-    scores = index_scores(True, meta, idx_queries, idx_weights.T, pieces)
-
-    def both_cores(arrays, units):
-        arrays = list(arrays) + [along(a, OVER_CORE) for a in arrays]
-        return arrays, units + [(device ^ 1, half, rel) for device, half, rel in units]
-
-    early, early_units = both_cores(
-        [value_maps, from_y, quarter],
-        [(0, 0, False), (0, 1, False), (2, 0, False), (2, 1, False)] + [(4 * z, 0, True) for z in (1, 2, 3)],
-    )
-    early_out = project(meta, back, latents, early_units, early)
-    late_in = [quarter_x, quarter_y, quarter_xy]
-    late, late_units = both_cores(
-        late_in,
-        [(4 * z, 1, True) for z in (1, 2, 3)]
-        + [(4 * z + 2, 0, True) for z in (1, 2, 3)]
-        + [(4 * z + 2, 1, True) for z in (1, 2, 3)],
-    )
-    attended = project(meta, back, latents, late_units, late, early_units, early_out, final=True)
+    late = [from_x, last_y, last_xy]
+    late_core = [along(a, OVER_CORE) for a in late]
+
+    early_units = [(0, 0, False), (0, 1, False), (2, 0, False), (2, 1, False)] + [(4 * z, 0, True) for z in (1, 2, 3)]
+    early_units = early_units + [(device ^ 1, half, rel) for device, half, rel in early_units]
+    early_out = project(meta, back, latents, early_units, early + early_core)
+    first_units = [(4 * z, 1, True) for z in (1, 2)] + [(4 * z + 2, 0, True) for z in (1, 2)]
+    late_units = [(4 * z + 2, 1, True) for z in (1, 2)] + [(12, 1, True), (14, 0, True), (14, 1, True)]
+    units = first_units + late_units
+    units = units + [(device ^ 1, half, rel) for device, half, rel in units]
+    arrays = [first_x, first_y] + late + first_core + late_core
+    attended = project(meta, back, latents, units, arrays, early_units, early_out, final=True)
     return (attended, scores)
 
 

time: 104 us -> 96 us (0.923)
  local copies, waits for them, and re-layouts: 14.9 us -> 6.4 us
  waiting for transfers between devices: 12 us -> 16.8 us
  starting transfers between devices: 21.4 us -> 17.4 us
    unnamed x18 -> x14, local copies, waits for them, and re-layouts: 11.7 us -> 4.48 us
    ppermute x17 -> x23, starting transfers between devices: 20.2 us -> 15.1 us  [along(): return lax.ppermute(array, 'ctx', pairs)]
    ppermute x17 -> x23, waiting for transfers between devices: 12 us -> 16.8 us  [along(): return lax.ppermute(array, 'ctx', pairs)]
    pallas_call x2, Pallas kernels: 8.75 us -> 5.61 us  [project(): pl.pallas_call(functools.partial(project_kernel, tuple(units), sizes, tup...]
    pallas_call x1, Pallas kernels: 27.5 us -> 29.9 us  [attend(): pl.pallas_call(functools.partial(attend_kernel, relative, len(pieces)), g...]
    ppermute x2 -> x3, starting transfers between devices: 1.19 us -> 2.29 us  [the longest x2 1.6 us: across(): return lax.ppermute(array, 'groups', [(0, 1), (1, 0)])]
  transfers between devices with their start and end apart: 19 -> 26, of which waited for: 5 -> 5; matrix products, arithmetic and copies ran while one was open for 8% -> 5% of each run, Pallas kernels for 44% -> 49%
where the time goes in v3:
time: 96 us; the launch traced here: 94.9 us
  Pallas kernels  50.2 us (52%)
  starting transfers between devices  17.4 us (18%)
  waiting for transfers between devices  16.8 us (18%)
  local copies, waits for them, and re-layouts  6.4 us (7%)
  other arithmetic  3.28 us (3%)
    pallas_call x1, Pallas kernels, attend(): pl.pallas_call(functools.partial(attend_kernel, relative, len(pieces)), g...  29.9 us
    ppermute x23, waiting for transfers between devices, along(): return lax.ppermute(array, 'ctx', pairs)  16.8 us
    ppermute x23, starting transfers between devices, along(): return lax.ppermute(array, 'ctx', pairs)  15.1 us
    pallas_call x1, Pallas kernels, index_scores(): pl.pallas_call(functools.partial(index_kernel, relative, len(pieces)), gr...  8.55 us
    pallas_call x1, Pallas kernels, sort_queries(): pl.pallas_call(sort_kernel, grid=(H // step,), in_specs=[pl.BlockSpec((co...  6.16 us
    pallas_call x2, Pallas kernels, project(): pl.pallas_call(functools.partial(project_kernel, tuple(units), sizes, tup...  5.61 us
    unnamed x14, local copies, waits for them, and re-layouts  4.48 us
  transfers between devices with their start and end apart: 26, of which 5 were waited for; matrix products, arithmetic and copies ran while one was open for 5% of the time, Pallas kernels for 49%

profile of v3, /device:TPU:31, one launch (start us, length us, event | category | flops | bytes accessed | tf_op | source)
XLA Modules:
  0.0 94.9 jit_solution(5650281514707281473)
XLA Ops:
  0.6 0.9 pad_maximum_fusion.2
  1.9 1.0 %constant_dynamic-slice_fusion = bf16[2,512,128]{2,1,0:T(8,128)(2,1)S(1)} fusion(bf16[4,512,128]{2,1,0:T(8,128)(2,1)} %refs_15_.1, s32[]{:T(128)S(6)} %select_n.40), kind=kLoop, calls=%fused_computation.35 | loop fusion | bytes 524292 | tf_op jit(solution)/shard_map/dynamic_slice | solution.py:341
  2.8 2.4 %collective-permute-start.1 = (bf16[2,512,128]{2,1,0:T(8,128)(2,1)S(1)}, bf16[2,512,128]{2,1,0:T(8,128)(2,1)S(1)}, u32[]{:S(2)}, u32[]{:S(2)}) collective-permute-start(bf16[2,512,128]{2,1,0:T(8,128)(2,1)S(1)} %constant_dynamic-slice_fusion), channel_id=1, source_target_pairs={{0,8},{1,9},{2,10},{3,11},{4,12},{5,13},{6,14},{7,15},{8,0},{9,1},... | collective-permute-start | bytes 786440 | tf_op jit(solution)/shard_map/ppermute | solution.py:318
  5.2 1.3 %collective-permute-start.4 = (bf16[2,512,128]{2,1,0:T(8,128)(2,1)S(1)}, bf16[2,512,128]{2,1,0:T(8,128)(2,1)S(1)}, u32[]{:S(2)}, u32[]{:S(2)}) collective-permute-start(bf16[2,512,128]{2,1,0:T(8,128)(2,1)S(1)} %constant_dynamic-slice_fusion), channel_id=1, source_target_pairs={{0,4},{1,5},{2,6},{3,7},{4,0},{5,1},{6,2},{7,3},{8,12},{9,13},{10,... | collective-permute-start | bytes 786440 | tf_op jit(solution)/shard_map/ppermute | solution.py:318
  6.7 0.8 constant_dynamic-update-slice_fusion.6
  7.5 0.7 fusion.6
  8.4 0.7 slice.30
  9.1 0.8 compare_or_fusion
  10.4 3.4 %collective-permute-done = bf16[704,128]{1,0:T(8,128)(2,1)S(1)} collective-permute-done((bf16[704,128]{1,0:T(8,128)(2,1)S(1)}, bf16[704,128]{1,0:T(8,128)(2,1)S(1)}, u32[]{:S(2)}, u32[]{:S(2)}) %collective-permute-start) | collective-permute-done | bytes 180256 | tf_op jit(solution)/shard_map/ppermute | solution.py:318
  13.9 10.2 %collective-permute-done.1 = bf16[2,512,128]{2,1,0:T(8,128)(2,1)S(1)} collective-permute-done((bf16[2,512,128]{2,1,0:T(8,128)(2,1)S(1)}, bf16[2,512,128]{2,1,0:T(8,128)(2,1)S(1)}, u32[]{:S(2)}, u32[]{:S(2)}) %collective-permute-start.1) | collective-permute-done | bytes 262176 | tf_op jit(solution)/shard_map/ppermute | solution.py:318
  24.3 0.3 collective-permute-start.5
  24.9 3.7 %copy-done = bf16[128,36864]{1,0:T(8,128)(2,1)S(1)} copy-done((bf16[128,36864]{1,0:T(8,128)(2,1)S(1)}, bf16[128,36864]{1,0:T(8,128)(2,1)}, u32[]{:S(2)}) %copy-start) | copy-done | bytes 9437208
  28.6 6.2 %sort_queries.1.q_ref = bf16[16,512,576]{2,1,0:T(8,128)(2,1)} custom-call(bf16[128,128]{1,0:T(8,128)(2,1)S(1)} %get-tuple-element.20.order_ref, bf16[128,36864]{1,0:T(8,128)(2,1)S(1)} %copy-done), custom_call_target="tpu_custom_call" | custom-call | flops 1 | bytes 1 | tf_op jit(solution)/shard_map/sort_queries/pallas_call | solution.py:41
  34.8 1.3 %collective-permute-start.11 = (bf16[512,128]{1,0:T(8,128)(2,1)S(1)}, bf16[512,128]{1,0:T(8,128)(2,1)S(1)}, u32[]{:S(2)}, u32[]{:S(2)}) collective-permute-start(bf16[512,128]{1,0:T(8,128)(2,1)S(1)} %pad_maximum_fusion.3), channel_id=1, source_target_pairs={{0,2},{1,3},{2,0},{3,1},{4,6},{5,7},{6,4},{7,5},{8,10},{9,11},{10,... | collective-permute-start | bytes 393224 | tf_op jit(solution)/shard_map/ppermute | solution.py:318
  36.2 1.9 %collective-permute-start.13 = (bf16[4,512,128]{2,1,0:T(8,128)(2,1)S(1)}, bf16[4,512,128]{2,1,0:T(8,128)(2,1)S(1)}, u32[]{:S(2)}, u32[]{:S(2)}) collective-permute-start(bf16[4,512,128]{2,1,0:T(8,128)(2,1)S(1)} %copy-done.1), channel_id=1, source_target_pairs={{0,1},{1,0},{2,3},{3,2},{4,5},{5,4},{6,7},{7,6},{8,9},{9,8},{10,11... | collective-permute-start | bytes 1572872 | tf_op jit(solution)/shard_map/ppermute | solution.py:318
  38.2 0.5 collective-permute-start.9
  38.6 1.8 %collective-permute-done.11 = bf16[512,128]{1,0:T(8,128)(2,1)S(1)} collective-permute-done((bf16[512,128]{1,0:T(8,128)(2,1)S(1)}, bf16[512,128]{1,0:T(8,128)(2,1)S(1)}, u32[]{:S(2)}, u32[]{:S(2)}) %collective-permute-start.11) | collective-permute-done | bytes 131104 | tf_op jit(solution)/shard_map/ppermute | solution.py:318
  40.5 1.9 %collective-permute-start.12 = (bf16[1024,128]{1,0:T(8,128)(2,1)S(1)}, bf16[1024,128]{1,0:T(8,128)(2,1)S(1)}, u32[]{:S(2)}, u32[]{:S(2)}) collective-permute-start(bf16[1024,128]{1,0:T(8,128)(2,1)S(1)} %constant_dynamic-update-slice_fusion.2), channel_id=1, source_target_pairs={{0,1},{1,0},{2,3},{3,2},{4,5},{5,4},{6,7},{7,6},{8,9},{9,8},{10,11... | collective-permute-start | bytes 786440 | tf_op jit(solution)/shard_map/ppermute | solution.py:318
  42.4 1.1 %collective-permute-done.12 = bf16[1024,128]{1,0:T(8,128)(2,1)S(1)} collective-permute-done((bf16[1024,128]{1,0:T(8,128)(2,1)S(1)}, bf16[1024,128]{1,0:T(8,128)(2,1)S(1)}, u32[]{:S(2)}, u32[]{:S(2)}) %collective-permute-start.12) | collective-permute-done | bytes 262176 | tf_op jit(solution)/shard_map/ppermute | solution.py:318
  43.5 0.4 collective-permute-start.16
  43.9 8.5 %index_scores.1 = f32[16,128]{1,0:T(8,128)} custom-call(s32[2]{0:T(128)S(1)} %pad_add_fusion.me_ref, bf16[128,4096]{1,0:T(8,128)(2,1)S(1)} %copy-done.2, f32[32,128]{1,0:T(8,128)S(1)} %bitcast.20, bf16[8,128,128]{2,1,0:T(8,128)(2,1)S(1)} %bitcast.18, bf16[8,128,128]{2,1,0:T(8,128)(2,1)S(1)} %bitcast.19), custom_call_target="tpu_custom_call" | custom-call | flops 1 | bytes 1 | tf_op jit(solution)/shard_map/index_scores/pallas_call | solution.py:294
  52.5 2.0 %collective-permute-start.17 = (bf16[2304,128]{1,0:T(8,128)(2,1)S(1)}, bf16[2304,128]{1,0:T(8,128)(2,1)S(1)}, u32[]{:S(2)}, u32[]{:S(2)}) collective-permute-start(bf16[2304,128]{1,0:T(8,128)(2,1)S(1)} %collective-permute-done.9), channel_id=1, source_target_pairs={{0,1},{1,0},{2,3},{3,2},{4,5},{5,4},{6,7},{7,6},{8,9},{9,8},{10,11... | collective-permute-start | bytes 1769480 | tf_op jit(solution)/shard_map/ppermute | solution.py:318
  54.5 1.3 %collective-permute-start.20 = (bf16[6,512,128]{2,1,0:T(8,128)(2,1)S(1)}, bf16[6,512,128]{2,1,0:T(8,128)(2,1)S(1)}, u32[]{:S(2)}, u32[]{:S(2)}) collective-permute-start(bf16[6,512,128]{2,1,0:T(8,128)(2,1)S(1)} %pad_maximum_fusion), channel_id=1, source_target_pairs={{0,16},{16,0},{1,17},{17,1},{2,18},{18,2},{3,19},{19,3},{4,20},{20... | collective-permute-start | bytes 2359304 | tf_op jit(solution)/shard_map/ppermute | solution.py:322
  55.8 0.3 collective-permute-start.18
  56.3 0.8 collective-permute-start.21
  57.1 0.7 collective-permute-start.22
  57.8 29.9 %attend.1.refs_1_.refs_2_.refs_3_.refs_4_.refs_5_.refs_6_.refs_7_.refs_8_.refs_9_.refs_10_.refs_11_.refs_12_.refs_13_.refs_14_.refs_15_.refs_16_.refs_17_.refs_18_ = bf16[64,128,512]{2,1,0:T(8,128)(2,1)S(1)} custom-call(s32[128]{0:T(128)S(1)} %convert_reduce_fusion.run_ref, s32[3]{0:T(128)S(1)} %convert_reduce_fusion.3.offset_ref, ...), custom_call_target="tpu_custom_call" | custom-call | flops 1 | bytes 1 | tf_op jit(solution)/shard_map/attend/pallas_call | solution.py:160
  87.7 0.9 collective-permute-start.23
  88.7 0.4 collective-permute-start.25
  89.1 1.9 %project.2.refs_29_ = bf16[128,3584]{1,0:T(8,128)(2,1)S(1)} custom-call(s32[2]{0:T(128)S(1)} %pad_add_fusion.me_ref, bf16[128,128]{1,0:T(8,128)(2,1)S(1)} %get-tuple-element.40.refs_0_, ...), custom_call_target="tpu_custom_call" | custom-call | flops 1 | bytes 1 | tf_op jit(solution)/shard_map/project/pallas_call | solution.py:226
  91.0 0.2 collective-permute-done.25.refs_28_
  91.2 3.7 %project.3 = bf16[128,8192]{1,0:T(8,128)(2,1)} custom-call(s32[2]{0:T(128)S(1)} %pad_add_fusion.me_ref, bf16[128,128]{1,0:T(8,128)(2,1)S(1)} %get-tuple-element.40.refs_0_, ...), custom_call_target="tpu_custom_call" | custom-call | flops 1 | bytes 1 | tf_op jit(solution)/shard_map/project/pallas_call | solution.py:226
  (65 shorter events, 2.5 us)
Async XLA Ops:
  1.6 12.3 %collective-permute-start = (bf16[704,128]{1,0:T(8,128)(2,1)S(1)}, bf16[704,128]{1,0:T(8,128)(2,1)S(1)}, u32[]{:S(2)}, u32[]{:S(2)}) collective-permute-start(bf16[704,128]{1,0:T(8,128)(2,1)S(1)} %pad_maximum_fusion.2), channel_id=1, source_target_pairs={{0,8},{1,9},{2,10},{3,11},{4,12},{5,13},{6,14},{7,15},{8,0},{9,1},... | collective-permute-start | bytes 540680 | tf_op jit(solution)/shard_map/ppermute | solution.py:318
  1.7 12.2 %collective-permute-start.2 = (bf16[704,128]{1,0:T(8,128)(2,1)S(1)}, bf16[704,128]{1,0:T(8,128)(2,1)S(1)}, u32[]{:S(2)}, u32[]{:S(2)}) collective-permute-start(bf16[704,128]{1,0:T(8,128)(2,1)S(1)} %pad_maximum_fusion.2), channel_id=1, source_target_pairs={{0,4},{1,5},{2,6},{3,7},{4,0},{5,1},{6,2},{7,3},{8,12},{9,13},{10,... | collective-permute-start | bytes 540680 | tf_op jit(solution)/shard_map/ppermute | solution.py:318
  2.8 21.2 %collective-permute-start.1 = (bf16[2,512,128]{2,1,0:T(8,128)(2,1)S(1)}, bf16[2,512,128]{2,1,0:T(8,128)(2,1)S(1)}, u32[]{:S(2)}, u32[]{:S(2)}) collective-permute-start(bf16[2,512,128]{2,1,0:T(8,128)(2,1)S(1)} %constant_dynamic-slice_fusion), channel_id=1, source_target_pairs={{0,8},{1,9},{2,10},{3,11},{4,12},{5,13},{6,14},{7,15},{8,0},{9,1},... | collective-permute-start | bytes 786440 | tf_op jit(solution)/shard_map/ppermute | solution.py:318
  5.2 19.0 %collective-permute-start.4 = (bf16[2,512,128]{2,1,0:T(8,128)(2,1)S(1)}, bf16[2,512,128]{2,1,0:T(8,128)(2,1)S(1)}, u32[]{:S(2)}, u32[]{:S(2)}) collective-permute-start(bf16[2,512,128]{2,1,0:T(8,128)(2,1)S(1)} %constant_dynamic-slice_fusion), channel_id=1, source_target_pairs={{0,4},{1,5},{2,6},{3,7},{4,0},{5,1},{6,2},{7,3},{8,12},{9,13},{10,... | collective-permute-start | bytes 786440 | tf_op jit(solution)/shard_map/ppermute | solution.py:318
  6.5 31.6 %collective-permute-start.8 = (bf16[4,512,128]{2,1,0:T(8,128)(2,1)}, bf16[4,512,128]{2,1,0:T(8,128)(2,1)S(1)}, u32[]{:S(2)}, u32[]{:S(2)}) collective-permute-start(bf16[4,512,128]{2,1,0:T(8,128)(2,1)} %refs_15_.1), channel_id=1, source_target_pairs={{0,2},{1,3},{2,0},{3,1},{4,6},{5,7},{6,4},{7,5},{8,10},{9,11},{10,... | collective-permute-start | bytes 1572872 | tf_op jit(solution)/shard_map/ppermute | solution.py:318
  13.8 20.9 %collective-permute-start.3 = (bf16[704,128]{1,0:T(8,128)(2,1)S(1)}, bf16[704,128]{1,0:T(8,128)(2,1)S(1)}, u32[]{:S(2)}, u32[]{:S(2)}) collective-permute-start(bf16[704,128]{1,0:T(8,128)(2,1)S(1)} %collective-permute-done), channel_id=1, source_target_pairs={{0,4},{1,5},{2,6},{3,7},{4,0},{5,1},{6,2},{7,3},{8,12},{9,13},{10,... | collective-permute-start | bytes 540680 | tf_op jit(solution)/shard_map/ppermute | solution.py:318
  24.3 10.5 %copy-start.5 = (bf16[128,128]{1,0:T(8,128)(2,1)S(1)}, bf16[128,128]{1,0:T(8,128)(2,1)}, u32[]{:S(2)}) copy-start(bf16[128,128]{1,0:T(8,128)(2,1)} %param.10) | copy-start | bytes 98308
  24.3 11.8 %copy-start.4 = (bf16[128,576]{0,1:T(8,128)(2,1)S(1)}, bf16[128,576]{0,1:T(8,128)(2,1)}, u32[]{:S(2)}) copy-start(bf16[128,576]{0,1:T(8,128)(2,1)} %param.8) | copy-start | bytes 442372
  24.3 13.8 %collective-permute-start.5 = (bf16[4,512,128]{2,1,0:T(8,128)(2,1)S(1)}, bf16[4,512,128]{2,1,0:T(8,128)(2,1)S(1)}, u32[]{:S(2)}, u32[]{:S(2)}) collective-permute-start(bf16[4,512,128]{2,1,0:T(8,128)(2,1)S(1)} %constant_dynamic-update-slice_fusion.refs_17_), channel_id=1, source_target_pairs={{0,16},{16,0},{1,17},{17,1},{2,18},{18,2},{3,19},{19,3},{4,20},{20... | collective-permute-start | bytes 1572872 | tf_op jit(solution)/shard_map/ppermute | solution.py:322
  24.7 13.5 %collective-permute-start.6 = (bf16[4,512,128]{2,1,0:T(8,128)(2,1)S(1)}, bf16[4,512,128]{2,1,0:T(8,128)(2,1)S(1)}, u32[]{:S(2)}, u32[]{:S(2)}) collective-permute-start(bf16[4,512,128]{2,1,0:T(8,128)(2,1)S(1)} %constant_dynamic-update-slice_fusion.refs_17_), channel_id=1, source_target_pairs={{0,2},{1,3},{2,0},{3,1},{4,6},{5,7},{6,4},{7,5},{8,10},{9,11},{10,... | collective-permute-start | bytes 1572872 | tf_op jit(solution)/shard_map/ppermute | solution.py:318
  24.9 11.3 %collective-permute-start.7 = (bf16[2,512,128]{2,1,0:T(8,128)(2,1)S(1)}, bf16[2,512,128]{2,1,0:T(8,128)(2,1)S(1)}, u32[]{:S(2)}, u32[]{:S(2)}) collective-permute-start(bf16[2,512,128]{2,1,0:T(8,128)(2,1)S(1)} %collective-permute-done.1), channel_id=1, source_target_pairs={{0,4},{1,5},{2,6},{3,7},{4,0},{5,1},{6,2},{7,3},{8,12},{9,13},{10,... | collective-permute-start | bytes 786440 | tf_op jit(solution)/shard_map/ppermute | solution.py:318
  24.9 3.7 %copy-start = (bf16[128,36864]{1,0:T(8,128)(2,1)S(1)}, bf16[128,36864]{1,0:T(8,128)(2,1)}, u32[]{:S(2)}) copy-start(bf16[128,36864]{1,0:T(8,128)(2,1)} %q_ref.2) | copy-start | bytes 28311556
  34.7 1.5 %copy-start.1 = (bf16[4,512,128]{2,1,0:T(8,128)(2,1)S(1)}, bf16[4,512,128]{2,1,0:T(8,128)(2,1)}, u32[]{:S(2)}) copy-start(bf16[4,512,128]{2,1,0:T(8,128)(2,1)} %refs_15_.1) | copy-start | bytes 1572868
  34.7 9.2 %copy-start.2 = (bf16[128,4096]{1,0:T(8,128)(2,1)S(1)}, bf16[128,4096]{1,0:T(8,128)(2,1)}, u32[]{:S(2)}) copy-start(bf16[128,4096]{1,0:T(8,128)(2,1)} %q_ref.3) | copy-start | bytes 3145732
  34.7 9.2 %copy-start.3 = (f32[128,32]{0,1:T(8,128)S(1)}, f32[128,32]{0,1:T(8,128)}, u32[]{:S(2)}) copy-start(f32[128,32]{0,1:T(8,128)} %param.11) | copy-start | bytes 49156
  34.8 5.6 %collective-permute-start.11 = (bf16[512,128]{1,0:T(8,128)(2,1)S(1)}, bf16[512,128]{1,0:T(8,128)(2,1)S(1)}, u32[]{:S(2)}, u32[]{:S(2)}) collective-permute-start(bf16[512,128]{1,0:T(8,128)(2,1)S(1)} %pad_maximum_fusion.3), channel_id=1, source_target_pairs={{0,2},{1,3},{2,0},{3,1},{4,6},{5,7},{6,4},{7,5},{8,10},{9,11},{10,... | collective-permute-start | bytes 393224 | tf_op jit(solution)/shard_map/ppermute | solution.py:318
  36.2 16.3 %collective-permute-start.13 = (bf16[4,512,128]{2,1,0:T(8,128)(2,1)S(1)}, bf16[4,512,128]{2,1,0:T(8,128)(2,1)S(1)}, u32[]{:S(2)}, u32[]{:S(2)}) collective-permute-start(bf16[4,512,128]{2,1,0:T(8,128)(2,1)S(1)} %copy-done.1), channel_id=1, source_target_pairs={{0,1},{1,0},{2,3},{3,2},{4,5},{5,4},{6,7},{7,6},{8,9},{9,8},{10,11... | collective-permute-start | bytes 1572872 | tf_op jit(solution)/shard_map/ppermute | solution.py:318
  38.1 14.4 %collective-permute-start.15 = (bf16[4,512,128]{2,1,0:T(8,128)(2,1)S(1)}, bf16[4,512,128]{2,1,0:T(8,128)(2,1)S(1)}, u32[]{:S(2)}, u32[]{:S(2)}) collective-permute-start(bf16[4,512,128]{2,1,0:T(8,128)(2,1)S(1)} %constant_dynamic-update-slice_fusion.refs_17_), channel_id=1, source_target_pairs={{0,1},{1,0},{2,3},{3,2},{4,5},{5,4},{6,7},{7,6},{8,9},{9,8},{10,11... | collective-permute-start | bytes 1572872 | tf_op jit(solution)/shard_map/ppermute | solution.py:318
  38.2 14.3 %collective-permute-start.9 = (bf16[2304,128]{1,0:T(8,128)(2,1)S(1)}, bf16[2304,128]{1,0:T(8,128)(2,1)S(1)}, u32[]{:S(2)}, u32[]{:S(2)}) collective-permute-start(bf16[2304,128]{1,0:T(8,128)(2,1)S(1)} %pad_maximum_fusion.1), channel_id=1, source_target_pairs={{0,2},{1,3},{2,0},{3,1},{4,6},{5,7},{6,4},{7,5},{8,10},{9,11},{10,... | collective-permute-start | bytes 1769480 | tf_op jit(solution)/shard_map/ppermute | solution.py:318
  40.5 3.1 %collective-permute-start.12 = (bf16[1024,128]{1,0:T(8,128)(2,1)S(1)}, bf16[1024,128]{1,0:T(8,128)(2,1)S(1)}, u32[]{:S(2)}, u32[]{:S(2)}) collective-permute-start(bf16[1024,128]{1,0:T(8,128)(2,1)S(1)} %constant_dynamic-update-slice_fusion.2), channel_id=1, source_target_pairs={{0,1},{1,0},{2,3},{3,2},{4,5},{5,4},{6,7},{7,6},{8,9},{9,8},{10,11... | collective-permute-start | bytes 786440 | tf_op jit(solution)/shard_map/ppermute | solution.py:318
  42.4 10.1 %collective-permute-start.14 = (bf16[4,512,128]{2,1,0:T(8,128)(2,1)S(1)}, bf16[4,512,128]{2,1,0:T(8,128)(2,1)S(1)}, u32[]{:S(2)}, u32[]{:S(2)}) collective-permute-start(bf16[4,512,128]{2,1,0:T(8,128)(2,1)S(1)} %collective-permute-done.8.refs_16_), channel_id=1, source_target_pairs={{0,1},{1,0},{2,3},{3,2},{4,5},{5,4},{6,7},{7,6},{8,9},{9,8},{10,11... | collective-permute-start | bytes 1572872 | tf_op jit(solution)/shard_map/ppermute | solution.py:318
  43.5 8.9 %collective-permute-start.16 = (bf16[2,512,128]{2,1,0:T(8,128)(2,1)S(1)}, bf16[2,512,128]{2,1,0:T(8,128)(2,1)S(1)}, u32[]{:S(2)}, u32[]{:S(2)}) collective-permute-start(bf16[2,512,128]{2,1,0:T(8,128)(2,1)S(1)} %collective-permute-done.7.refs_18_), channel_id=1, source_target_pairs={{0,1},{1,0},{2,3},{3,2},{4,5},{5,4},{6,7},{7,6},{8,9},{9,8},{10,11... | collective-permute-start | bytes 786440 | tf_op jit(solution)/shard_map/ppermute | solution.py:318
  52.4 3.9 %collective-permute-start.10 = (bf16[2304,128]{1,0:T(8,128)(2,1)S(1)}, bf16[2304,128]{1,0:T(8,128)(2,1)S(1)}, u32[]{:S(2)}, u32[]{:S(2)}) collective-permute-start(bf16[2304,128]{1,0:T(8,128)(2,1)S(1)} %pad_maximum_fusion.1), channel_id=1, source_target_pairs={{0,1},{1,0},{2,3},{3,2},{4,5},{5,4},{6,7},{7,6},{8,9},{9,8},{10,11... | collective-permute-start | bytes 1769480 | tf_op jit(solution)/shard_map/ppermute | solution.py:318
  52.5 4.6 %collective-permute-start.17 = (bf16[2304,128]{1,0:T(8,128)(2,1)S(1)}, bf16[2304,128]{1,0:T(8,128)(2,1)S(1)}, u32[]{:S(2)}, u32[]{:S(2)}) collective-permute-start(bf16[2304,128]{1,0:T(8,128)(2,1)S(1)} %collective-permute-done.9), channel_id=1, source_target_pairs={{0,1},{1,0},{2,3},{3,2},{4,5},{5,4},{6,7},{7,6},{8,9},{9,8},{10,11... | collective-permute-start | bytes 1769480 | tf_op jit(solution)/shard_map/ppermute | solution.py:318
  54.5 33.2 %collective-permute-start.20 = (bf16[6,512,128]{2,1,0:T(8,128)(2,1)S(1)}, bf16[6,512,128]{2,1,0:T(8,128)(2,1)S(1)}, u32[]{:S(2)}, u32[]{:S(2)}) collective-permute-start(bf16[6,512,128]{2,1,0:T(8,128)(2,1)S(1)} %pad_maximum_fusion), channel_id=1, source_target_pairs={{0,16},{16,0},{1,17},{17,1},{2,18},{18,2},{3,19},{19,3},{4,20},{20... | collective-permute-start | bytes 2359304 | tf_op jit(solution)/shard_map/ppermute | solution.py:322
  55.8 31.9 %collective-permute-start.18 = (bf16[4,512,128]{2,1,0:T(8,128)(2,1)S(1)}, bf16[4,512,128]{2,1,0:T(8,128)(2,1)S(1)}, u32[]{:S(2)}, u32[]{:S(2)}) collective-permute-start(bf16[4,512,128]{2,1,0:T(8,128)(2,1)S(1)} %collective-permute-done.5.refs_19_), channel_id=1, source_target_pairs={{0,1},{1,0},{2,3},{3,2},{4,5},{5,4},{6,7},{7,6},{8,9},{9,8},{10,11... | collective-permute-start | bytes 1572872 | tf_op jit(solution)/shard_map/ppermute | solution.py:318
  56.1 31.6 %collective-permute-start.19 = (bf16[4,512,128]{2,1,0:T(8,128)(2,1)S(1)}, bf16[4,512,128]{2,1,0:T(8,128)(2,1)S(1)}, u32[]{:S(2)}, u32[]{:S(2)}) collective-permute-start(bf16[4,512,128]{2,1,0:T(8,128)(2,1)S(1)} %collective-permute-done.6.refs_20_), channel_id=1, source_target_pairs={{0,1},{1,0},{2,3},{3,2},{4,5},{5,4},{6,7},{7,6},{8,9},{9,8},{10,11... | collective-permute-start | bytes 1572872 | tf_op jit(solution)/shard_map/ppermute | solution.py:318
  56.3 31.4 %collective-permute-start.21 = (bf16[2,512,128]{2,1,0:T(8,128)(2,1)S(1)}, bf16[2,512,128]{2,1,0:T(8,128)(2,1)S(1)}, u32[]{:S(2)}, u32[]{:S(2)}) collective-permute-start(bf16[2,512,128]{2,1,0:T(8,128)(2,1)S(1)} %collective-permute-done.7.refs_18_), channel_id=1, source_target_pairs={{0,2},{1,3},{2,0},{3,1},{4,6},{5,7},{6,4},{7,5},{8,10},{9,11},{10,... | collective-permute-start | bytes 786440 | tf_op jit(solution)/shard_map/ppermute | solution.py:318
  57.1 30.6 %collective-permute-start.22 = (bf16[2,512,128]{2,1,0:T(8,128)(2,1)S(1)}, bf16[2,512,128]{2,1,0:T(8,128)(2,1)S(1)}, u32[]{:S(2)}, u32[]{:S(2)}) collective-permute-start(bf16[2,512,128]{2,1,0:T(8,128)(2,1)S(1)} %collective-permute-done.7.refs_18_), channel_id=1, source_target_pairs={{0,18},{1,19},{2,16},{3,17},{4,22},{5,23},{6,20},{7,21},{8,26},{9,... | collective-permute-start | bytes 786440 | tf_op jit(solution)/shard_map/ppermute | solution.py:394
  87.7 3.5 %collective-permute-start.23 = (bf16[6,512,128]{2,1,0:T(8,128)(2,1)S(1)}, bf16[6,512,128]{2,1,0:T(8,128)(2,1)S(1)}, u32[]{:S(2)}, u32[]{:S(2)}) collective-permute-start(bf16[6,512,128]{2,1,0:T(8,128)(2,1)S(1)} %collective-permute-done.20.refs_21_), channel_id=1, source_target_pairs={{0,1},{1,0},{2,3},{3,2},{4,5},{5,4},{6,7},{7,6},{8,9},{9,8},{10,11... | collective-permute-start | bytes 2359304 | tf_op jit(solution)/shard_map/ppermute | solution.py:318
  88.6 2.4 %collective-permute-start.24 = (bf16[2,512,128]{2,1,0:T(8,128)(2,1)S(1)}, bf16[2,512,128]{2,1,0:T(8,128)(2,1)S(1)}, u32[]{:S(2)}, u32[]{:S(2)}) collective-permute-start(bf16[2,512,128]{2,1,0:T(8,128)(2,1)S(1)} %collective-permute-done.21.refs_22_), channel_id=1, source_target_pairs={{0,1},{1,0},{2,3},{3,2},{4,5},{5,4},{6,7},{7,6},{8,9},{9,8},{10,11... | collective-permute-start | bytes 786440 | tf_op jit(solution)/shard_map/ppermute | solution.py:318
  88.7 2.6 %collective-permute-start.25 = (bf16[2,512,128]{2,1,0:T(8,128)(2,1)S(1)}, bf16[2,512,128]{2,1,0:T(8,128)(2,1)S(1)}, u32[]{:S(2)}, u32[]{:S(2)}) collective-permute-start(bf16[2,512,128]{2,1,0:T(8,128)(2,1)S(1)} %collective-permute-done.22.refs_23_), channel_id=1, source_target_pairs={{0,1},{1,0},{2,3},{3,2},{4,5},{5,4},{6,7},{7,6},{8,9},{9,8},{10,11... | collective-permute-start | bytes 786440 | tf_op jit(solution)/shard_map/ppermute | solution.py:318
